TPU v7x, 32 devices: a whole 2x2x4 slice. The times are simulated.
32 devices in a mesh: probe: 4 (over y, x), space: 8 (over z, core).
Axes of the slice: x: 2, y: 2, z: 4, core: 2. Of those that a mesh axis runs over, the one named last changes fastest.
Arguments:
- probes: float32 [128, 32768], P('probe', 'space'), may hold values from -6 to 6
- sensitivity: float32 [8, 8, 16384], P(None, None, 'space'), may hold values from -2.1 to 2.1
- obs_weight: float32 [8, 16384], P(None, 'space'), may hold values from 0.5 to 4
- prior_weight: float32 [32768], P('space'), may hold values from 0.2 to 2
- connectivity: int32 [8, 16384], P(None, 'space'), may hold values from 0 to 4351, as said below
Outputs:
- basis: float32 [128, 32768], P('probe', 'space')
- factor: float32 [128, 128], replicated
Inputs may be any that keep to these rules, and one draw needn't show every extreme that they name: Each column holds 8 distinct numbers. For an element of the block of device d of space (columns d * 2048 to (d + 1) * 2048 - 1), connectivity + d * 4096 - 128 is an existing node, and the values 0 and 4351 are both named wherever those nodes exist.
All inputs are finite; a program needn't handle non-finite values.
Results may differ from a plain program's by a relative error of at most 0.0003.
Values sent between devices are 32-bit elements; how exact they have to be, the bound alone decides.
A program may use at most 64 MiB of HBM per device.

v0:
```python
import math

import jax
import jax.numpy as jnp
from jax import lax
from jax.sharding import PartitionSpec as P

HALO = 128


highest = lax.Precision.HIGHEST


def extended_2(block, sides, width):
    for axis, dim in sides:
        count = lax.axis_size(axis)
        forward = [(i, i + 1) for i in range(count - 1)]
        backward = [(target, source) for source, target in forward]
        low = lax.ppermute(
            lax.slice_in_dim(block, block.shape[dim] - width, None, axis=dim), axis, forward
        )
        high = lax.ppermute(lax.slice_in_dim(block, 0, width, axis=dim), axis, backward)
        block = jnp.concatenate([low, block, high], axis=dim)
    return block


def shifted(block, axis, distance):
    devices = range(lax.axis_size(axis))
    route = [(i - distance, i) for i in devices if i - distance in devices]
    return lax.ppermute(block, axis, route)


def element_images(extended, sensitivity, obs_weight, local):
    gathered = extended[:, local]
    gauss_count = sensitivity.shape[0]
    corner_count = sensitivity.shape[1]
    observed = []
    for gauss in range(gauss_count):
        total = gathered[:, 0, :] * sensitivity[gauss, 0][None, :]
        for corner in range(1, corner_count):
            total = total + gathered[:, corner, :] * sensitivity[gauss, corner][None, :]
        observed.append(total * obs_weight[gauss][None, :])
    pulled = []
    for corner in range(corner_count):
        total = observed[0] * sensitivity[0, corner][None, :]
        for gauss in range(1, gauss_count):
            total = total + observed[gauss] * sensitivity[gauss, corner][None, :]
        pulled.append(total)
    pulled = jnp.stack(pulled, axis=1)
    return jnp.zeros(extended.shape, jnp.float32).at[:, local].add(pulled)


def gram_over_space(partial_value):
    return lax.psum(partial_value, "space")


def orthonormal(rows, reduce_gram):
    gram_first = reduce_gram(
        jnp.dot(rows, rows.T, precision=highest, preferred_element_type=jnp.float32)
    )
    lower_first = jnp.linalg.cholesky(gram_first)
    basis_first = lax.linalg.triangular_solve(lower_first, rows, left_side=True, lower=True)
    gram_second = reduce_gram(
        jnp.dot(basis_first, basis_first.T, precision=highest, preferred_element_type=jnp.float32)
    )
    lower_second = jnp.linalg.cholesky(gram_second)
    basis = lax.linalg.triangular_solve(lower_second, basis_first, left_side=True, lower=True)
    factor = jnp.dot(
        lower_first, lower_second, precision=highest, preferred_element_type=jnp.float32
    ).T
    return (basis, factor)


def on_device(probes, sensitivity, obs_weight, prior_weight, connectivity):
    node_count = probes.shape[1]
    probe_count = probes.shape[0]
    extended = extended_2(probes, (("space", 1),), HALO)
    summed = element_images(extended, sensitivity, obs_weight, connectivity)
    lower_rim = shifted(summed[:, :HALO], "space", -1)
    upper_rim = shifted(summed[:, HALO + node_count :], "space", 1)
    images = summed[:, HALO : HALO + node_count] + prior_weight[None, :] * probes
    images = images.at[:, node_count - HALO :].add(lower_rim)
    images = images.at[:, :HALO].add(upper_rim)
    scale = math.sqrt(float(node_count * lax.axis_size("space")))
    whole = lax.all_gather(images, "probe", axis=0, tiled=True)
    basis, factor = orthonormal(whole, gram_over_space)
    basis = lax.dynamic_slice_in_dim(basis, lax.axis_index("probe") * probe_count, probe_count, 0)
    return (basis * scale, factor / scale)


def solution(mesh):
    return jax.shard_map(
        on_device,
        mesh=mesh,
        in_specs=(
            P("probe", "space"),
            P(None, None, "space"),
            P(None, "space"),
            P("space"),
            P(None, "space"),
        ),
        out_specs=(P("probe", "space"), P()),
        check_vma=False,
    )
```

profile of v0, /device:TPU:0, one launch (start us, length us, event | category | flops | bytes accessed | tf_op | source)
XLA Modules:
  0.0 417.6 jit_solution(15581203816817797125)
XLA Ops:
  8.0 2.3 collective-permute-start
  11.7 1.7 fusion.28
  15.1 1.7 fusion.26
  20.2 3.0 copy.52
  24.6 54.8 %gather_fusion = f32[16384,32]{1,0:T(8,128)} fusion(f32[32,4352]{0,1:T(8,128)S(1)} %copy.40, s32[16384]{0:T(1024)S(1)} %broadcast_clamp_fusion), kind=kCustom, calls=%fused_computation | custom fusion | bytes 4259840 | tf_op jit(solution)/shard_map/gather | solution.py:34
  79.3 5.1 %copy.42 = f32[8,2048,32]{1,2,0:T(8,128)S(1)} copy(f32[8,2048,32]{2,1,0:T(8,128)} %bitcast.103) | data formatting | bytes 4194304 | tf_op jit(solution)/shard_map/gather | solution.py:34
  84.4 1.7 multiply_add_fusion
  91.9 5.1 %stack.2 = f32[32,8,2048]{2,1,0:T(8,128)S(1)} concatenate(f32[32,1,2048]{2,1,0:T(1,128)} %copy.43, f32[32,1,2048]{2,1,0:T(1,128)} %copy.44, f32[32,1,2048]{2,1,0:T(1,128)S(1)} %copy.45, f32[32,1,2048]{2,1,0:T(1,128)S(1)} %copy.46, f32[32,1,2048]{2,1,0:T(1,128)S(1)} %copy.47, f32[32,1,2048]{2,1,0:T(1,128)S(1)} %copy.48, f32[32,1,2048]{2,1,0:T(1,128)S(1)} %copy.49, ...), dimensions={1} | concatenate | bytes 4194304 | tf_op jit(solution)/shard_map/stack | solution.py:49
  97.0 4.6 %copy.62 = f32[8,2048,32]{2,1,0:T(8,128)} copy(f32[8,2048,32]{1,0,2:T(8,128)S(1)} %bitcast.106) | data formatting | bytes 4194304 | tf_op jit(solution)/shard_map/stack | solution.py:49
  101.7 88.2 %scatter_custom_fusion = f32[32,4352]{0,1:T(8,128)S(1)} fusion(s32[16384]{0:T(1024)S(1)} %bitcast.108, f32[16384,32]{1,0:T(8,128)} %bitcast.104, f32[]{:T(128)} %constant.95.clone.1), kind=kCustom, calls=%fused_computation.4 | custom fusion | flops 524288 | bytes 557568 | tf_op jit(solution)/shard_map/scatter-add | solution.py:50
  191.2 5.8 %collective-permute-start.3 = (f32[32,128]{0,1:T(8,128)S(1)}, f32[32,128]{0,1:T(8,128)S(1)}, u32[]{:S(2)}, u32[]{:S(2)}) collective-permute-start(f32[32,128]{0,1:T(8,128)S(1)} %get-tuple-element.37), channel_id=1, source_target_pairs={{0,1},{1,2},{2,3},{3,4},{4,5},{5,6},{6,7},{8,9},{9,10},{10,11},{11... | collective-permute-start | bytes 49160 | tf_op jit(solution)/shard_map/ppermute | solution.py:30
  197.1 2.5 slice_add_fusion
  201.8 37.8 %all-gather.2.cloned.1.call-done = f32[128,4096]{1,0:T(8,128)} async-done(((f32[32,4096]{1,0:T(8,128)}), f32[128,4096]{1,0:T(8,128)}) %all-gather.2.cloned.1.call-update) | async-done | bytes 2097168 | tf_op jit(solution)/shard_map/all_gather | solution.py:85
  239.6 4.7 %fusion.32 = f32[128,128]{0,1:T(8,128)} fusion(f32[128,4096]{1,0:T(8,128)} %all-gather.2.cloned.1.call-done), kind=kOutput, calls=%fused_computation.65 | convolution fusion | flops 805306368 | bytes 2162688 | tf_op jit(solution)/shard_map/dot_general | solution.py:59
  244.5 53.5 %all-reduce.3.cloned.1.call-done = f32[128,128]{0,1:T(8,128)} async-done(((f32[128,128]{0,1:T(8,128)}), f32[128,128]{0,1:T(8,128)}) %all-reduce.3.cloned.1.call-update) | async-done | bytes 65552 | tf_op jit(solution)/shard_map/psum | solution.py:54
  299.8 11.7 %cholesky.44 = f32[128,128]{1,0:T(8,128)S(1)} custom-call(f32[128,128]{1,0:T(8,128)S(1)} %fusion.10), custom_call_target="Cholesky" | custom-call | tf_op jit(solution)/shard_map/jit(cholesky)/cholesky | solution.py:61
  312.8 9.8 %custom-call.6 = f32[1,128,128]{1,2,0:T(8,128)S(1)} custom-call(f32[1,128,128]{2,1,0:T(8,128)S(1)} %fusion.14), custom_call_target="InvertDiagBlocksLowerTriangular" | custom-call | tf_op jit(solution)/shard_map/triangular_solve/custom-call.0 | solution.py:62
  322.7 3.5 fusion.8
  326.2 2.4 fusion.33
  328.6 52.7 %all-reduce.5.cloned.1.call-done = f32[128,128]{0,1:T(8,128)} async-done(((f32[128,128]{0,1:T(8,128)}), f32[128,128]{0,1:T(8,128)}) %all-reduce.5.cloned.1.call-update) | async-done | bytes 65552 | tf_op jit(solution)/shard_map/psum | solution.py:54
  383.2 11.9 %cholesky.55 = f32[128,128]{1,0:T(8,128)S(1)} custom-call(f32[128,128]{1,0:T(8,128)S(1)} %fusion.7), custom_call_target="Cholesky" | custom-call | tf_op jit(solution)/shard_map/jit(cholesky)/cholesky | solution.py:66
  395.7 2.1 convolution_multiply_fusion
  398.4 9.8 %custom-call.7 = f32[1,128,128]{1,2,0:T(8,128)S(1)} custom-call(f32[1,128,128]{2,1,0:T(8,128)S(1)} %select_bitcast_fusion), custom_call_target="InvertDiagBlocksLowerTriangular" | custom-call | tf_op jit(solution)/shard_map/triangular_solve/custom-call.0 | solution.py:67
  408.3 1.9 fusion.5
  (58 shorter events, 25.0 us)
Async XLA Ops:
  7.2 232.4 %all-gather.2.cloned.1.call-start = ((), (), s32[]{:S(2)}) async-start(), calls=%async_computation | async-start | bytes 2621440 | tf_op jit(solution)/shard_map/all_gather | solution.py:85
  8.0 15.9 %collective-permute-start = (f32[32,128]{1,0:T(8,128)S(1)}, f32[32,128]{1,0:T(8,128)S(1)}, u32[]{:S(2)}, u32[]{:S(2)}) collective-permute-start(f32[32,128]{1,0:T(8,128)S(1)} %get-tuple-element.103), channel_id=1, source_target_pairs={{0,1},{1,2},{2,3},{3,4},{4,5},{5,6},{6,7},{8,9},{9,10},{10,11},{11... | collective-permute-start | bytes 49160 | tf_op jit(solution)/shard_map/ppermute | solution.py:19
  10.3 13.6 %copy-start.1 = (f32[32,4096]{1,0:T(8,128)S(1)}, f32[32,4096]{1,0:T(8,128)}, u32[]{:S(2)}) copy-start(f32[32,4096]{1,0:T(8,128)} %param.12) | copy-start | bytes 1572868
  10.3 13.6 %collective-permute-start.1 = (f32[32,128]{1,0:T(8,128)S(1)}, f32[32,128]{1,0:T(8,128)S(1)}, u32[]{:S(2)}, u32[]{:S(2)}) collective-permute-start(f32[32,128]{1,0:T(8,128)S(1)} %get-tuple-element.104), channel_id=1, source_target_pairs={{1,0},{2,1},{3,2},{4,3},{5,4},{6,5},{7,6},{9,8},{10,9},{11,10},{12... | collective-permute-start | bytes 49160 | tf_op jit(solution)/shard_map/ppermute | solution.py:22
  101.7 95.4 %copy-start.2 = (f32[4096]{0:T(1024)S(1)}, f32[4096]{0:T(1024)}, u32[]{:S(2)}) copy-start(f32[4096]{0:T(1024)} %param.15) | copy-start | bytes 49156
  189.9 1.4 copy-start
  189.9 9.7 %collective-permute-start.2 = (f32[32,128]{0,1:T(8,128)S(1)}, f32[32,128]{0,1:T(8,128)S(1)}, u32[]{:S(2)}, u32[]{:S(2)}) collective-permute-start(f32[32,128]{0,1:T(8,128)S(1)} %get-tuple-element.38), channel_id=1, source_target_pairs={{1,0},{2,1},{3,2},{4,3},{5,4},{6,5},{7,6},{9,8},{10,9},{11,10},{12... | collective-permute-start | bytes 49160 | tf_op jit(solution)/shard_map/ppermute | solution.py:30
  191.2 8.4 %collective-permute-start.3 = (f32[32,128]{0,1:T(8,128)S(1)}, f32[32,128]{0,1:T(8,128)S(1)}, u32[]{:S(2)}, u32[]{:S(2)}) collective-permute-start(f32[32,128]{0,1:T(8,128)S(1)} %get-tuple-element.37), channel_id=1, source_target_pairs={{0,1},{1,2},{2,3},{3,4},{4,5},{5,6},{6,7},{8,9},{9,10},{10,11},{11... | collective-permute-start | bytes 49160 | tf_op jit(solution)/shard_map/ppermute | solution.py:30
  201.7 96.3 %all-reduce.3.cloned.1.call-start = ((), (), s32[]{:S(2)}) async-start(), calls=%async_computation.1 | async-start | bytes 131072 | tf_op jit(solution)/shard_map/psum | solution.py:54
  244.3 137.1 %all-reduce.5.cloned.1.call-start = ((), (), s32[]{:S(2)}) async-start(), calls=%async_computation.2 | async-start | bytes 131072 | tf_op jit(solution)/shard_map/psum | solution.py:54
Sparse Core Ops, SparseCore 0:
  201.8 37.6 all-gather.1
  244.4 53.5 all-reduce.2
  328.7 52.5 all-reduce.4
where the time goes:
time: 419 us; the launch traced here: 418 us
  other arithmetic  144 us (34%)
  waiting for transfers between devices  144 us (34%)
  local copies, waits for them, and re-layouts  89.1 us (21%)
  matrix products  14.7 us (4%)
  between operations  14 us (3%)
  starting transfers between devices  11.2 us (3%)
    psum x2, waiting for transfers between devices, gram_over_space(): return lax.psum(partial_value, 'space')  106 us
    scatter-add x1, other arithmetic, element_images(): return jnp.zeros(extended.shape, jnp.float32).at[:, local].add(pulled)  88.2 us
    gather x2, local copies, waits for them, and re-layouts, element_images(): gathered = extended[:, local]  59.9 us
    all_gather x1, waiting for transfers between devices, on_device(): whole = lax.all_gather(images, 'probe', axis=0, tiled=True)  37.8 us
    another operation x3, other arithmetic, orthonormal(): lower_second = jnp.linalg.cholesky(gram_second)  12.6 us
    another operation x3, other arithmetic, orthonormal(): lower_first = jnp.linalg.cholesky(gram_first)  12.4 us
    another operation x2, other arithmetic, orthonormal(): lax.linalg.triangular_solve(lower_first, rows, left_side=True, lower=True)  10.5 us
    another operation x2, other arithmetic, orthonormal(): lax.linalg.triangular_solve(lower_second, basis_first, left_side=True, lo...  10.4 us
  transfers between devices with their start and end apart: 7, of which 3 were waited for; matrix products, arithmetic and copies ran while one was open for 4% of the time, Pallas kernels for 0%

commit v1 on v0

--- a/solution.py
+++ b/solution.py
@@ -3,6 +3,8 @@
 import jax
 import jax.numpy as jnp
 from jax import lax
+from jax.experimental import pallas as pl
+from jax.experimental.pallas import tpu as pltpu
 from jax.sharding import PartitionSpec as P
 
 HALO = 128
@@ -30,24 +32,128 @@
     return lax.ppermute(block, axis, route)
 
 
+TILE = 128
+WIDE = 256
+
+
+def split_exact(value):
+    high = value.astype(jnp.bfloat16)
+    rest = value - high.astype(jnp.float32)
+    middle = rest.astype(jnp.bfloat16)
+    low = (rest - middle.astype(jnp.float32)).astype(jnp.bfloat16)
+    return high, middle, low
+
+
+def element_kernel(extended, local, sensitivity, weight, out, node, held, pulled, total):
+    gauss_count, corner_count, element_count = sensitivity.shape
+    rows, nodes = extended.shape
+    tiles, wides = nodes // TILE, nodes // WIDE
+    total[...] = jnp.zeros_like(total)
+
+    def block(step, carry):
+        start = pl.multiple_of(step * WIDE, WIDE)
+        for c in range(corner_count):
+            index = local[c : c + 1, pl.ds(start, WIDE)]
+            node[c] = jnp.broadcast_to(index, (8, WIDE))
+
+        def gather(corner, carry):
+            for part in range(WIDE // TILE):
+                index = node[corner, :, part * TILE : (part + 1) * TILE]
+                lane, tile = index & (TILE - 1), index >> 7
+                found = [jnp.zeros((8, TILE), jnp.float32)] * (rows // 8)
+                for t in range(tiles):
+                    here = tile == t
+                    for r in range(rows // 8):
+                        source = extended[r * 8 : (r + 1) * 8, t * TILE : (t + 1) * TILE]
+                        picked = jnp.take_along_axis(
+                            source, lane, axis=1, mode="promise_in_bounds"
+                        )
+                        found[r] = jnp.where(here, picked, found[r])
+                for r in range(rows // 8):
+                    held[corner, r * 8 : (r + 1) * 8, part * TILE : (part + 1) * TILE] = found[r]
+            return carry
+
+        lax.fori_loop(0, corner_count, gather, 0)
+
+        for part in range(WIDE // TILE):
+            lanes = slice(part * TILE, (part + 1) * TILE)
+            place = pl.multiple_of(start + part * TILE, TILE)
+            for r in range(rows // 16):
+                band = slice(r * 16, (r + 1) * 16)
+                values = [held[c, band, lanes] for c in range(corner_count)]
+                sums = [None] * corner_count
+                for g in range(gauss_count):
+                    coefficient = [
+                        sensitivity[g, c : c + 1, pl.ds(place, TILE)] for c in range(corner_count)
+                    ]
+                    observed = values[0] * coefficient[0]
+                    for c in range(1, corner_count):
+                        observed = observed + values[c] * coefficient[c]
+                    observed = observed * weight[g : g + 1, pl.ds(place, TILE)]
+                    for c in range(corner_count):
+                        term = observed * coefficient[c]
+                        sums[c] = term if g == 0 else sums[c] + term
+                for c in range(corner_count):
+                    pulled[c, band, lanes] = sums[c]
+
+        def scatter(corner, carry):
+            index = node[corner, 0:1, :]
+            lane = jnp.broadcast_to(index & (WIDE - 1), (WIDE, WIDE))
+            wide = jnp.broadcast_to(index >> 8, (16, WIDE))
+            hot = jnp.where(lax.broadcasted_iota(jnp.int32, (WIDE, WIDE), 0) == lane, 1.0, 0.0)
+            hot = hot.astype(jnp.bfloat16)
+            hot = jnp.concatenate([hot, hot, hot], axis=1)
+            value = jnp.concatenate(split_exact(pulled[corner]), axis=1)
+            masked = []
+            for h in range(wides):
+                mask = jnp.where(wide == h, 1.0, 0.0).astype(jnp.bfloat16)
+                mask = jnp.concatenate([mask] * (rows // 16), axis=0)
+                masked.append(value * jnp.concatenate([mask] * 3, axis=1))
+            masked = jnp.concatenate(masked, axis=0)
+            total[...] += lax.dot_general(
+                masked, hot, (((1,), (1,)), ((), ())), preferred_element_type=jnp.float32
+            )
+            return carry
+
+        lax.fori_loop(0, corner_count, scatter, 0)
+        return carry
+
+    lax.fori_loop(0, element_count // WIDE, block, 0)
+    for h in range(wides):
+        out[:, h * WIDE : (h + 1) * WIDE] = total[h * rows : (h + 1) * rows, :]
+
+
+def padded(array, dim, multiple):
+    extra = -array.shape[dim] % multiple
+    if not extra:
+        return array
+    return jnp.pad(array, [(0, extra if d == dim else 0) for d in range(array.ndim)])
+
+
 def element_images(extended, sensitivity, obs_weight, local):
-    gathered = extended[:, local]
-    gauss_count = sensitivity.shape[0]
-    corner_count = sensitivity.shape[1]
-    observed = []
-    for gauss in range(gauss_count):
-        total = gathered[:, 0, :] * sensitivity[gauss, 0][None, :]
-        for corner in range(1, corner_count):
-            total = total + gathered[:, corner, :] * sensitivity[gauss, corner][None, :]
-        observed.append(total * obs_weight[gauss][None, :])
-    pulled = []
-    for corner in range(corner_count):
-        total = observed[0] * sensitivity[0, corner][None, :]
-        for gauss in range(1, gauss_count):
-            total = total + observed[gauss] * sensitivity[gauss, corner][None, :]
-        pulled.append(total)
-    pulled = jnp.stack(pulled, axis=1)
-    return jnp.zeros(extended.shape, jnp.float32).at[:, local].add(pulled)
+    probe_count, node_count = extended.shape
+    corner_count = local.shape[0]
+    extended = padded(padded(extended, 0, 16), 1, WIDE)
+    local = padded(local, 1, WIDE)
+    sensitivity = padded(sensitivity, 2, WIDE)
+    obs_weight = padded(obs_weight, 1, WIDE)
+    rows, nodes = extended.shape
+    vmem = pl.BlockSpec(memory_space=pltpu.VMEM)
+    summed = pl.pallas_call(
+        element_kernel,
+        out_shape=jax.ShapeDtypeStruct((rows, nodes), jnp.float32),
+        in_specs=[vmem] * 4,
+        out_specs=vmem,
+        scratch_shapes=[
+            pltpu.VMEM((corner_count, 8, WIDE), jnp.int32),
+            pltpu.VMEM((corner_count, rows, WIDE), jnp.float32),
+            pltpu.VMEM((corner_count, rows, WIDE), jnp.float32),
+            pltpu.VMEM((nodes // WIDE * rows, WIDE), jnp.float32),
+        ],
+        compiler_params=pltpu.CompilerParams(vmem_limit_bytes=48 * 1024 * 1024),
+        name="elements",
+    )(extended, local, sensitivity, obs_weight)
+    return summed[:probe_count, :node_count]
 
 
 def gram_over_space(partial_value):

time: 419 us -> 299 us (0.71)
  other arithmetic: 144 us -> 50.8 us
  local copies, waits for them, and re-layouts: 89.1 us -> 6.16 us
  Pallas kernels: 0 us -> 53.4 us
  waiting for transfers between devices: 144 us -> 149 us
    scatter-add x1 -> x0, other arithmetic: 88.2 us -> none  [element_images(): return jnp.zeros(extended.shape, jnp.float32).at[:, local].add(pulled)]
    gather x2 -> x0, local copies, waits for them, and re-layouts: 59.9 us -> none  [element_images(): gathered = extended[:, local]]
    pallas_call x0 -> x1, Pallas kernels: none -> 53.4 us  [element_images(): pl.pallas_call(element_kernel, out_shape=jax.ShapeDtypeStruct((rows, node...]
    another operation x2 -> x0, local copies, waits for them, and re-layouts: 9.73 us -> none  [element_images(): pulled = jnp.stack(pulled, axis=1)]
    slice x5 -> x0, local copies, waits for them, and re-layouts: 7.53 us -> none  [the longest x3 4.58 us: element_images(): total = gathered[:, 0, :] * sensitivity[gauss, 0][None, :]]
    add x8 -> x0, local copies, waits for them, and re-layouts: 4.26 us -> none  [element_images(): total = total + observed[gauss] * sensitivity[gauss, corner][None, :]]
  transfers between devices with their start and end apart: 7 -> 7, of which waited for: 3 -> 5; matrix products, arithmetic and copies ran while one was open for 4% -> 0% of each run, Pallas kernels for 0% -> 0%
where the time goes in v1:
time: 299 us
  waiting for transfers between devices  149 us (50%)
  Pallas kernels  53.4 us (18%)
  other arithmetic  50.8 us (17%)
  matrix products  14.6 us (5%)
  between operations  14 us (5%)
  starting transfers between devices  10.2 us (3%)
  local copies, waits for them, and re-layouts  6.16 us (2%)
    psum x2, waiting for transfers between devices, gram_over_space(): return lax.psum(partial_value, 'space')  106 us
    pallas_call x1, Pallas kernels, element_images(): pl.pallas_call(element_kernel, out_shape=jax.ShapeDtypeStruct((rows, node...  53.4 us
    all_gather x1, waiting for transfers between devices, on_device(): whole = lax.all_gather(images, 'probe', axis=0, tiled=True)  39 us
    another operation x3, other arithmetic, orthonormal(): lower_second = jnp.linalg.cholesky(gram_second)  12.6 us
    another operation x3, other arithmetic, orthonormal(): lower_first = jnp.linalg.cholesky(gram_first)  12.4 us
    another operation x2, other arithmetic, orthonormal(): lax.linalg.triangular_solve(lower_first, rows, left_side=True, lower=True)  10.5 us
    another operation x2, other arithmetic, orthonormal(): lax.linalg.triangular_solve(lower_second, basis_first, left_side=True, lo...  10.4 us
    ppermute x2, starting transfers between devices, shifted(): return lax.ppermute(block, axis, route)  6.3 us
  transfers between devices with their start and end apart: 7, of which 5 were waited for; matrix products, arithmetic and copies ran while one was open for 0% of the time, Pallas kernels for 0%

profile of v1, /device:TPU:0, one launch (start us, length us, event | category | flops | bytes accessed | tf_op | source)
XLA Modules:
  0.0 298.7 jit_solution(4831568144614184781)
XLA Ops:
  8.0 2.3 collective-permute-start
  10.4 1.3 collective-permute-start.1
  12.3 3.3 %collective-permute-done.1 = f32[32,128]{1,0:T(8,128)S(1)} collective-permute-done((f32[32,128]{1,0:T(8,128)S(1)}, f32[32,128]{1,0:T(8,128)S(1)}, u32[]{:S(2)}, u32[]{:S(2)}) %collective-permute-start.1) | collective-permute-done | bytes 16416 | tf_op jit(solution)/shard_map/ppermute | solution.py:24
  15.6 1.1 pad_maximum_fusion.extended
  16.7 1.0 copy-done
  19.4 53.4 %elements.1 = f32[32,4352]{1,0:T(8,128)S(1)} custom-call(f32[32,4352]{1,0:T(8,128)S(1)} %pad_maximum_fusion.extended, s32[8,2048]{1,0:T(8,128)S(1)} %copy-done.1, f32[8,8,2048]{2,1,0:T(8,128)S(1)} %copy-done, f32[8,2048]{1,0:T(8,128)S(1)} %copy-done.2), custom_call_target="tpu_custom_call" | custom-call | tf_op jit(solution)/shard_map/elements/pallas_call | solution.py:142
  72.9 1.3 collective-permute-start.2
  74.3 5.0 %collective-permute-start.3 = (f32[32,128]{1,0:T(8,128)S(1)}, f32[32,128]{1,0:T(8,128)S(1)}, u32[]{:S(2)}, u32[]{:S(2)}) collective-permute-start(f32[32,128]{1,0:T(8,128)S(1)} %get-tuple-element.28), channel_id=1, source_target_pairs={{0,1},{1,2},{2,3},{3,4},{4,5},{5,6},{6,7},{8,9},{9,10},{10,11},{11... | collective-permute-start | bytes 49160 | tf_op jit(solution)/shard_map/ppermute | solution.py:32
  81.6 39.0 %all-gather.2.cloned.1.call-done = f32[128,4096]{1,0:T(8,128)} async-done(((f32[32,4096]{1,0:T(8,128)}), f32[128,4096]{1,0:T(8,128)}) %all-gather.2.cloned.1.call-update) | async-done | bytes 2097168 | tf_op jit(solution)/shard_map/all_gather | solution.py:191
  120.7 4.7 %fusion.24 = f32[128,128]{0,1:T(8,128)} fusion(f32[128,4096]{1,0:T(8,128)} %all-gather.2.cloned.1.call-done), kind=kOutput, calls=%fused_computation.37 | convolution fusion | flops 805306368 | bytes 2162688 | tf_op jit(solution)/shard_map/dot_general | solution.py:165
  125.6 53.5 %all-reduce.3.cloned.1.call-done = f32[128,128]{0,1:T(8,128)} async-done(((f32[128,128]{0,1:T(8,128)}), f32[128,128]{0,1:T(8,128)}) %all-reduce.3.cloned.1.call-update) | async-done | bytes 65552 | tf_op jit(solution)/shard_map/psum | solution.py:160
  179.1 0.9 copy.8
  180.1 0.9 fusion.5
  180.9 11.7 %cholesky.44 = f32[128,128]{1,0:T(8,128)S(1)} custom-call(f32[128,128]{1,0:T(8,128)S(1)} %fusion.5), custom_call_target="Cholesky" | custom-call | tf_op jit(solution)/shard_map/jit(cholesky)/cholesky | solution.py:167
  194.0 9.8 %custom-call.6 = f32[1,128,128]{1,2,0:T(8,128)S(1)} custom-call(f32[1,128,128]{2,1,0:T(8,128)S(1)} %fusion.9), custom_call_target="InvertDiagBlocksLowerTriangular" | custom-call | tf_op jit(solution)/shard_map/triangular_solve/custom-call.0 | solution.py:168
  203.8 3.5 %fusion.3 = f32[128,4096]{1,0:T(8,128)S(1)} fusion(f32[128,4096]{1,0:T(8,128)} %all-gather.2.cloned.1.call-done, f32[1,128,128]{1,2,0:T(8,128)S(1)} %custom-call.6), kind=kOutput, calls=%fused_computation.8 | convolution fusion | flops 805306368 | bytes 4259840 | tf_op jit(solution)/shard_map/triangular_solve/dot.1 | solution.py:168
  207.3 2.4 fusion.25
  209.7 52.8 %all-reduce.5.cloned.1.call-done = f32[128,128]{0,1:T(8,128)} async-done(((f32[128,128]{0,1:T(8,128)}), f32[128,128]{0,1:T(8,128)}) %all-reduce.5.cloned.1.call-update) | async-done | bytes 65552 | tf_op jit(solution)/shard_map/psum | solution.py:160
  262.5 0.9 copy.10
  263.4 0.9 fusion.2
  264.3 11.9 %cholesky.55 = f32[128,128]{1,0:T(8,128)S(1)} custom-call(f32[128,128]{1,0:T(8,128)S(1)} %fusion.2), custom_call_target="Cholesky" | custom-call | tf_op jit(solution)/shard_map/jit(cholesky)/cholesky | solution.py:172
  276.9 2.1 convolution_multiply_fusion
  279.6 9.8 %custom-call.7 = f32[1,128,128]{1,2,0:T(8,128)S(1)} custom-call(f32[1,128,128]{2,1,0:T(8,128)S(1)} %select_bitcast_fusion), custom_call_target="InvertDiagBlocksLowerTriangular" | custom-call | tf_op jit(solution)/shard_map/triangular_solve/custom-call.0 | solution.py:173
  289.4 1.9 fusion
  (33 shorter events, 9.2 us)
Async XLA Ops:
  7.2 67.0 %copy-start.3 = (f32[32,4096]{1,0:T(8,128)S(1)}, f32[32,4096]{1,0:T(8,128)}, u32[]{:S(2)}) copy-start(f32[32,4096]{1,0:T(8,128)} %param.12) | copy-start | bytes 1572868
  7.2 67.0 %copy-start.5 = (f32[4096]{0:T(1024)S(1)}, f32[4096]{0:T(1024)}, u32[]{:S(2)}) copy-start(f32[4096]{0:T(1024)} %param.15) | copy-start | bytes 49156
  7.2 113.5 %all-gather.2.cloned.1.call-start = ((), (), s32[]{:S(2)}) async-start(), calls=%async_computation | async-start | bytes 2621440 | tf_op jit(solution)/shard_map/all_gather | solution.py:191
  8.0 4.3 %collective-permute-start = (f32[32,128]{1,0:T(8,128)S(1)}, f32[32,128]{1,0:T(8,128)S(1)}, u32[]{:S(2)}, u32[]{:S(2)}) collective-permute-start(f32[32,128]{1,0:T(8,128)S(1)} %get-tuple-element.30), channel_id=1, source_target_pairs={{0,1},{1,2},{2,3},{3,4},{4,5},{5,6},{6,7},{8,9},{9,10},{10,11},{11... | collective-permute-start | bytes 49160 | tf_op jit(solution)/shard_map/ppermute | solution.py:21
  10.4 5.3 %collective-permute-start.1 = (f32[32,128]{1,0:T(8,128)S(1)}, f32[32,128]{1,0:T(8,128)S(1)}, u32[]{:S(2)}, u32[]{:S(2)}) collective-permute-start(f32[32,128]{1,0:T(8,128)S(1)} %get-tuple-element.31), channel_id=1, source_target_pairs={{1,0},{2,1},{3,2},{4,3},{5,4},{6,5},{7,6},{9,8},{10,9},{11,10},{12... | collective-permute-start | bytes 49160 | tf_op jit(solution)/shard_map/ppermute | solution.py:24
  16.7 1.0 copy-start
  17.8 0.8 copy-start.1
  18.6 0.8 copy-start.2
  72.9 6.4 %collective-permute-start.2 = (f32[32,128]{1,0:T(8,128)S(1)}, f32[32,128]{1,0:T(8,128)S(1)}, u32[]{:S(2)}, u32[]{:S(2)}) collective-permute-start(f32[32,128]{1,0:T(8,128)S(1)} %get-tuple-element.29), channel_id=1, source_target_pairs={{1,0},{2,1},{3,2},{4,3},{5,4},{6,5},{7,6},{9,8},{10,9},{11,10},{12... | collective-permute-start | bytes 49160 | tf_op jit(solution)/shard_map/ppermute | solution.py:32
  74.3 5.8 %collective-permute-start.3 = (f32[32,128]{1,0:T(8,128)S(1)}, f32[32,128]{1,0:T(8,128)S(1)}, u32[]{:S(2)}, u32[]{:S(2)}) collective-permute-start(f32[32,128]{1,0:T(8,128)S(1)} %get-tuple-element.28), channel_id=1, source_target_pairs={{0,1},{1,2},{2,3},{3,4},{4,5},{5,6},{6,7},{8,9},{9,10},{10,11},{11... | collective-permute-start | bytes 49160 | tf_op jit(solution)/shard_map/ppermute | solution.py:32
  80.8 0.8 copy-start.4
  81.6 97.5 %all-reduce.3.cloned.1.call-start = ((), (), s32[]{:S(2)}) async-start(), calls=%async_computation.1 | async-start | bytes 131072 | tf_op jit(solution)/shard_map/psum | solution.py:160
  125.4 137.1 %all-reduce.5.cloned.1.call-start = ((), (), s32[]{:S(2)}) async-start(), calls=%async_computation.2 | async-start | bytes 131072 | tf_op jit(solution)/shard_map/psum | solution.py:160
Sparse Core Ops, SparseCore 0:
  81.7 38.9 all-gather.1
  125.5 53.5 all-reduce.2
  209.9 52.6 all-reduce.4

commit v2 on v1

--- a/solution.py
+++ b/solution.py
@@ -1,3 +1,4 @@
+import functools
 import math
 
 import jax
@@ -24,12 +25,6 @@
         high = lax.ppermute(lax.slice_in_dim(block, 0, width, axis=dim), axis, backward)
         block = jnp.concatenate([low, block, high], axis=dim)
     return block
-
-
-def shifted(block, axis, distance):
-    devices = range(lax.axis_size(axis))
-    route = [(i - distance, i) for i in devices if i - distance in devices]
-    return lax.ppermute(block, axis, route)
 
 
 TILE = 128
@@ -156,42 +151,256 @@
     return summed[:probe_count, :node_count]
 
 
-def gram_over_space(partial_value):
-    return lax.psum(partial_value, "space")
-
-
-def orthonormal(rows, reduce_gram):
-    gram_first = reduce_gram(
-        jnp.dot(rows, rows.T, precision=highest, preferred_element_type=jnp.float32)
+MESH = pl.DeviceIdType.MESH
+BAND = 8
+
+
+def exact_dot(left, right, left_dim=1, right_dim=0):
+    return lax.dot_general(
+        left,
+        right,
+        (((left_dim,), (right_dim,)), ((), ())),
+        precision=highest,
+        preferred_element_type=jnp.float32,
     )
-    lower_first = jnp.linalg.cholesky(gram_first)
-    basis_first = lax.linalg.triangular_solve(lower_first, rows, left_side=True, lower=True)
-    gram_second = reduce_gram(
-        jnp.dot(basis_first, basis_first.T, precision=highest, preferred_element_type=jnp.float32)
+
+
+def small_factor(columns):
+    entry = {}
+    for m in range(BAND):
+        for i in range(m, BAND):
+            entry[i, m] = jnp.broadcast_to(columns[m][i : i + 1, :], columns[m].shape)
+    inverse = {}
+    for m in range(BAND):
+        root = lax.rsqrt(entry[m, m])
+        for i in range(m + 1, BAND):
+            entry[i, m] = entry[i, m] * root
+        for i in range(m + 1, BAND):
+            for k in range(m + 1, i + 1):
+                entry[i, k] = entry[i, k] - entry[i, m] * entry[k, m]
+        for k in range(m):
+            term = entry[m, k] * inverse[k, k]
+            for n in range(k + 1, m):
+                term = term + entry[m, n] * inverse[n, k]
+            inverse[m, k] = -term * root
+        inverse[m, m] = root
+    return inverse
+
+
+def factored(gram):
+    size = gram.shape[0]
+    row = lax.broadcasted_iota(jnp.int32, (size, size), 0)
+    column = lax.broadcasted_iota(jnp.int32, (size, size), 1)
+    unit = jnp.where(row == column, 1.0, 0.0)
+    level = lax.broadcasted_iota(jnp.int32, (BAND, size), 0)
+    bands = []
+    for j in range(size // BAND):
+        part = slice(j * BAND, (j + 1) * BAND)
+        bands.append((gram[part], unit[part]))
+    for j in range(size // BAND):
+        left, right = bands[j]
+        columns = [
+            jnp.broadcast_to(left[:, j * BAND + m : j * BAND + m + 1], left.shape)
+            for m in range(BAND)
+        ]
+        inverse = small_factor(columns)
+        new_left = new_right = None
+        for m in range(BAND):
+            weights = jnp.zeros_like(left)
+            for i in range(m, BAND):
+                weights = jnp.where(level == i, inverse[i, m], weights)
+            add_left = weights * left[m : m + 1, :]
+            add_right = weights * right[m : m + 1, :]
+            new_left = add_left if m == 0 else new_left + add_left
+            new_right = add_right if m == 0 else new_right + add_right
+        bands[j] = (new_left, new_right)
+        if (j + 1) * BAND < size:
+            multipliers = new_left.T
+            away_left = exact_dot(multipliers, new_left)
+            away_right = exact_dot(multipliers, new_right)
+            for i in range(j + 1, size // BAND):
+                part = slice(i * BAND, (i + 1) * BAND)
+                bands[i] = (bands[i][0] - away_left[part], bands[i][1] - away_right[part])
+    upper = jnp.concatenate([band[0] for band in bands], axis=0)
+    lower = jnp.concatenate([band[1] for band in bands], axis=0)
+    return jnp.where(row <= column, upper, 0.0), lower
+
+
+def send_all(axis, count, me, source, target, send_sem, recv_sem):
+    copies = []
+    for d in range(1, count):
+        to = lax.rem(me + d, count)
+        copy = pltpu.make_async_remote_copy(
+            src_ref=source(to),
+            dst_ref=target,
+            send_sem=send_sem.at[d],
+            recv_sem=recv_sem.at[d],
+            device_id={axis: to},
+            device_id_type=MESH,
+        )
+        copy.start()
+        copies.append(copy)
+    return copies
+
+
+def wait_all(copies):
+    for copy in copies:
+        copy.wait()
+
+
+def orthonormal_kernel(
+    probe_axis_size, space_axis_size, summed, probes, prior, basis, factor,
+    images, rim, mine, block, ready, partial, strips, bands, grams,
+    rim_send, rim_recv, move_send, move_recv, a_send, a_recv, b_send, b_recv, c_send, c_recv,
+):
+    p_me, s_me = lax.axis_index("probe"), lax.axis_index("space")
+    rows, nodes = probes.shape
+    size = rows * probe_axis_size
+    share = nodes // probe_axis_size
+    strip = size // space_axis_size
+    halo = (summed.shape[1] - nodes) // 2
+    scale = math.sqrt(float(nodes * space_axis_size))
+
+    barrier = pltpu.get_barrier_semaphore()
+    for d in range(1, space_axis_size):
+        to = lax.rem(s_me + d, space_axis_size)
+        pl.semaphore_signal(barrier, inc=1, device_id={"space": to}, device_id_type=MESH)
+    for d in range(1, probe_axis_size):
+        to = lax.rem(p_me + d, probe_axis_size)
+        pl.semaphore_signal(barrier, inc=1, device_id={"probe": to}, device_id_type=MESH)
+    pl.semaphore_wait(barrier, space_axis_size + probe_axis_size - 2)
+
+    def rim_copy(side):
+        source = summed.at[:, :halo] if side == 0 else summed.at[:, halo + nodes :]
+        return pltpu.make_async_remote_copy(
+            src_ref=source,
+            dst_ref=rim.at[side],
+            send_sem=rim_send.at[side],
+            recv_sem=rim_recv.at[side],
+            device_id={"space": s_me - 1 if side == 0 else s_me + 1},
+            device_id_type=MESH,
+        )
+
+    has_lower, has_upper = s_me > 0, s_me < space_axis_size - 1
+    pl.when(has_lower)(lambda: rim_copy(0).start())
+    pl.when(has_upper)(lambda: rim_copy(1).start())
+    images[...] = summed[:, halo : halo + nodes] + prior[...] * probes[...]
+
+    @pl.when(has_upper)
+    def _():
+        rim_copy(0).wait_recv()
+        images[:, nodes - halo :] += rim[0]
+
+    @pl.when(has_lower)
+    def _():
+        rim_copy(1).wait_recv()
+        images[:, :halo] += rim[1]
+
+    def lanes(index):
+        return pl.ds(pl.multiple_of(index * share, share), share)
+
+    copies = send_all(
+        "probe", probe_axis_size, p_me, lambda to: images.at[:, lanes(to)],
+        mine.at[p_me], move_send.at[0], move_recv.at[0],
     )
-    lower_second = jnp.linalg.cholesky(gram_second)
-    basis = lax.linalg.triangular_solve(lower_second, basis_first, left_side=True, lower=True)
-    factor = jnp.dot(
-        lower_first, lower_second, precision=highest, preferred_element_type=jnp.float32
-    ).T
-    return (basis, factor)
+    mine[p_me] = images[:, lanes(p_me)]
+    wait_all(copies)
+
+    def summed_gram(turn, value):
+        for s in range(space_axis_size):
+            partial[turn, s] = value[s * strip : (s + 1) * strip]
+        copies = send_all(
+            "space", space_axis_size, s_me, lambda to: partial.at[turn, to],
+            strips.at[turn, s_me], a_send.at[turn], a_recv.at[turn],
+        )
+        strips[turn, s_me] = partial[turn, s_me]
+        wait_all(copies)
+        total = strips[turn, 0]
+        for s in range(1, space_axis_size):
+            total = total + strips[turn, s]
+        bands[turn, p_me] = total
+        copies = send_all(
+            "probe", probe_axis_size, p_me, lambda to: bands.at[turn, p_me],
+            bands.at[turn, p_me], b_send.at[turn], b_recv.at[turn],
+        )
+        wait_all(copies)
+        total = bands[turn, 0]
+        for p in range(1, probe_axis_size):
+            total = total + bands[turn, p]
+        grams[turn, s_me] = total
+        copies = send_all(
+            "space", space_axis_size, s_me, lambda to: grams.at[turn, s_me],
+            grams.at[turn, s_me], c_send.at[turn], c_recv.at[turn],
+        )
+        wait_all(copies)
+        return jnp.concatenate([grams[turn, s] for s in range(space_axis_size)], axis=0)
+
+    whole = mine[...].reshape(size, share)
+    upper_first, inverse_first = factored(summed_gram(0, exact_dot(whole, whole, 1, 1)))
+    block[...] = exact_dot(inverse_first, mine[...].reshape(size, share))
+    first = block[...]
+    upper_second, inverse_second = factored(summed_gram(1, exact_dot(first, first, 1, 1)))
+    done = exact_dot(inverse_second * scale, block[...])
+    ready[...] = done.reshape(probe_axis_size, rows, share)
+    copies = send_all(
+        "probe", probe_axis_size, p_me, lambda to: ready.at[to],
+        basis.at[:, lanes(p_me)], move_send.at[1], move_recv.at[1],
+    )
+    basis[:, lanes(p_me)] = ready[p_me]
+    factor[...] = exact_dot(upper_second, upper_first) / scale
+    wait_all(copies)
+    pl.when(has_lower)(lambda: rim_copy(0).wait_send())
+    pl.when(has_upper)(lambda: rim_copy(1).wait_send())
+
+
+def orthonormal(summed, probes, prior):
+    probe_axis_size, space_axis_size = lax.axis_size("probe"), lax.axis_size("space")
+    rows, nodes = probes.shape
+    halo = (summed.shape[1] - nodes) // 2
+    size, share = rows * probe_axis_size, nodes // probe_axis_size
+    strip = size // space_axis_size
+    vmem = pl.BlockSpec(memory_space=pltpu.VMEM)
+    dma = pltpu.SemaphoreType.DMA
+    return pl.pallas_call(
+        functools.partial(orthonormal_kernel, probe_axis_size, space_axis_size),
+        out_shape=(
+            jax.ShapeDtypeStruct((rows, nodes), jnp.float32),
+            jax.ShapeDtypeStruct((size, size), jnp.float32),
+        ),
+        in_specs=[vmem] * 3,
+        out_specs=(vmem, vmem),
+        scratch_shapes=[
+            pltpu.VMEM((rows, nodes), jnp.float32),
+            pltpu.VMEM((2, rows, halo), jnp.float32),
+            pltpu.VMEM((probe_axis_size, rows, share), jnp.float32),
+            pltpu.VMEM((size, share), jnp.float32),
+            pltpu.VMEM((probe_axis_size, rows, share), jnp.float32),
+            pltpu.VMEM((2, space_axis_size, strip, size), jnp.float32),
+            pltpu.VMEM((2, space_axis_size, strip, size), jnp.float32),
+            pltpu.VMEM((2, probe_axis_size, strip, size), jnp.float32),
+            pltpu.VMEM((2, space_axis_size, strip, size), jnp.float32),
+            dma((2,)),
+            dma((2,)),
+            dma((2, probe_axis_size)),
+            dma((2, probe_axis_size)),
+            dma((2, space_axis_size)),
+            dma((2, space_axis_size)),
+            dma((2, probe_axis_size)),
+            dma((2, probe_axis_size)),
+            dma((2, space_axis_size)),
+            dma((2, space_axis_size)),
+        ],
+        compiler_params=pltpu.CompilerParams(
+            collective_id=0, has_side_effects=True, vmem_limit_bytes=48 * 1024 * 1024
+        ),
+        name="orthonormal",
+    )(summed, probes, prior)
 
 
 def on_device(probes, sensitivity, obs_weight, prior_weight, connectivity):
-    node_count = probes.shape[1]
-    probe_count = probes.shape[0]
     extended = extended_2(probes, (("space", 1),), HALO)
     summed = element_images(extended, sensitivity, obs_weight, connectivity)
-    lower_rim = shifted(summed[:, :HALO], "space", -1)
-    upper_rim = shifted(summed[:, HALO + node_count :], "space", 1)
-    images = summed[:, HALO : HALO + node_count] + prior_weight[None, :] * probes
-    images = images.at[:, node_count - HALO :].add(lower_rim)
-    images = images.at[:, :HALO].add(upper_rim)
-    scale = math.sqrt(float(node_count * lax.axis_size("space")))
-    whole = lax.all_gather(images, "probe", axis=0, tiled=True)
-    basis, factor = orthonormal(whole, gram_over_space)
-    basis = lax.dynamic_slice_in_dim(basis, lax.axis_index("probe") * probe_count, probe_count, 0)
-    return (basis * scale, factor / scale)
+    return orthonormal(summed, probes, prior_weight[None, :])
 
 
 def solution(mesh):

time: 299 us -> 128 us (0.43)
  waiting for transfers between devices: 149 us -> 3.96 us
  Pallas kernels: 53.4 us -> 116 us
  other arithmetic: 50.8 us -> 1.08 us
  matrix products: 14.6 us -> 0 us
  between operations: 14 us -> 0.75 us
  starting transfers between devices: 10.2 us -> 3.77 us
  local copies, waits for them, and re-layouts: 6.16 us -> 2.2 us
    psum x2 -> x0, waiting for transfers between devices: 106 us -> none  [gram_over_space(): return lax.psum(partial_value, 'space')]
    pallas_call x0 -> x1, Pallas kernels: none -> 63 us  [orthonormal(): pl.pallas_call(functools.partial(orthonormal_kernel, probe_axis_size, spa...]
    another operation x11 -> x0, other arithmetic: 46.5 us -> none  [the longest x3 12.6 us: orthonormal(): lower_second = jnp.linalg.cholesky(gram_second)]
    all_gather x1 -> x0, waiting for transfers between devices: 39 us -> none  [on_device(): whole = lax.all_gather(images, 'probe', axis=0, tiled=True)]
    dot_general x3 -> x0, matrix products: 9.23 us -> none  [the longest x1 4.68 us: orthonormal(): jnp.dot(rows, rows.T, precision=highest, preferred_element_type=jnp.float32)]
    ppermute x2 -> x0, starting transfers between devices: 6.3 us -> none  [shifted(): return lax.ppermute(block, axis, route)]
    another operation x2 -> x0, matrix products: 5.42 us -> none  [the longest x1 3.48 us: orthonormal(): lax.linalg.triangular_solve(lower_first, rows, left_side=True, lower=True)]
  transfers between devices with their start and end apart: 7 -> 2, of which waited for: 5 -> 1; matrix products, arithmetic and copies ran while one was open for 0% -> 0% of each run, Pallas kernels for 0% -> 0%
where the time goes in v2:
time: 128 us
  Pallas kernels  116 us (91%)
  waiting for transfers between devices  3.96 us (3%)
  starting transfers between devices  3.77 us (3%)
  local copies, waits for them, and re-layouts  2.2 us (2%)
    pallas_call x1, Pallas kernels, orthonormal(): pl.pallas_call(functools.partial(orthonormal_kernel, probe_axis_size, spa...  63 us
    pallas_call x1, Pallas kernels, element_images(): pl.pallas_call(element_kernel, out_shape=jax.ShapeDtypeStruct((rows, node...  53.4 us
    ppermute x1, waiting for transfers between devices, extended_2(): lax.ppermute(lax.slice_in_dim(block, 0, width, axis=dim), axis, backward)  3.96 us
  transfers between devices with their start and end apart: 2, of which 1 were waited for; matrix products, arithmetic and copies ran while one was open for 0% of the time, Pallas kernels for 0%

profile of v2, /device:TPU:0, one launch (start us, length us, event | category | flops | bytes accessed | tf_op | source)
XLA Modules:
  0.0 128.2 jit_solution(7332878372910723373)
XLA Ops:
  0.6 0.7 fusion
  1.4 2.3 %collective-permute-start = (f32[32,128]{1,0:T(8,128)S(1)}, f32[32,128]{1,0:T(8,128)S(1)}, u32[]{:S(2)}, u32[]{:S(2)}) collective-permute-start(f32[32,128]{1,0:T(8,128)S(1)} %get-tuple-element.2), channel_id=1, source_target_pairs={{0,1},{1,2},{2,3},{3,4},{4,5},{5,6},{6,7},{8,9},{9,10},{10,11},{11... | collective-permute-start | bytes 49160 | tf_op jit(solution)/shard_map/ppermute | solution.py:22
  3.7 0.0 copy-start.1
  3.7 0.0 copy-start.2
  3.7 0.0 copy-start.3
  3.8 1.4 %collective-permute-start.1 = (f32[32,128]{1,0:T(8,128)S(1)}, f32[32,128]{1,0:T(8,128)S(1)}, u32[]{:S(2)}, u32[]{:S(2)}) collective-permute-start(f32[32,128]{1,0:T(8,128)S(1)} %get-tuple-element.3), channel_id=1, source_target_pairs={{1,0},{2,1},{3,2},{4,3},{5,4},{6,5},{7,6},{9,8},{10,9},{11,10},{12... | collective-permute-start | bytes 49160 | tf_op jit(solution)/shard_map/ppermute | solution.py:25
  5.2 0.0 collective-permute-done
  5.2 4.0 %collective-permute-done.1 = f32[32,128]{1,0:T(8,128)S(1)} collective-permute-done((f32[32,128]{1,0:T(8,128)S(1)}, f32[32,128]{1,0:T(8,128)S(1)}, u32[]{:S(2)}, u32[]{:S(2)}) %collective-permute-start.1) | collective-permute-done | bytes 16416 | tf_op jit(solution)/shard_map/ppermute | solution.py:25
  9.2 1.1 pad_maximum_fusion.extended
  10.2 0.0 copy-done.1
  10.3 0.0 copy-done.2
  10.3 0.0 copy-done.3
  10.3 0.0 copy-start
  10.3 0.0 copy-start.4
  10.3 53.4 %elements.1.summed = f32[32,4352]{1,0:T(8,128)S(1)} custom-call(f32[32,4352]{1,0:T(8,128)S(1)} %pad_maximum_fusion.extended, s32[8,2048]{1,0:T(8,128)S(1)} %copy-done.2, f32[8,8,2048]{2,1,0:T(8,128)S(1)} %copy-done.1, f32[8,2048]{1,0:T(8,128)S(1)} %copy-done.3), custom_call_target="tpu_custom_call" | custom-call | tf_op jit(solution)/shard_map/elements/pallas_call | solution.py:137
  63.7 0.0 copy-done
  63.7 0.0 copy-done.4
  63.8 63.0 %orthonormal.1 = (f32[32,4096]{1,0:T(8,128)S(1)}, f32[128,128]{1,0:T(8,128)S(1)}) custom-call(f32[32,4352]{1,0:T(8,128)S(1)} %elements.1.summed, f32[32,4096]{1,0:T(8,128)S(1)} %copy-done, f32[1,4096]{1,0:T(1,128)S(1)} %bitcast.1), custom_call_target="tpu_custom_call" | custom-call | tf_op jit(solution)/shard_map/orthonormal/pallas_call | solution.py:364
  126.8 0.8 copy.9
  127.6 0.6 copy.10
Async XLA Ops:
  1.4 3.8 %collective-permute-start = (f32[32,128]{1,0:T(8,128)S(1)}, f32[32,128]{1,0:T(8,128)S(1)}, u32[]{:S(2)}, u32[]{:S(2)}) collective-permute-start(f32[32,128]{1,0:T(8,128)S(1)} %get-tuple-element.2), channel_id=1, source_target_pairs={{0,1},{1,2},{2,3},{3,4},{4,5},{5,6},{6,7},{8,9},{9,10},{10,11},{11... | collective-permute-start | bytes 49160 | tf_op jit(solution)/shard_map/ppermute | solution.py:22
  3.7 6.5 %copy-start.1 = (f32[8,8,2048]{2,1,0:T(8,128)S(1)}, f32[8,8,2048]{2,1,0:T(8,128)}, u32[]{:S(2)}) copy-start(f32[8,8,2048]{2,1,0:T(8,128)} %sensitivity.1) | copy-start | bytes 1572868
  3.7 6.5 %copy-start.2 = (s32[8,2048]{1,0:T(8,128)S(1)}, s32[8,2048]{1,0:T(8,128)}, u32[]{:S(2)}) copy-start(s32[8,2048]{1,0:T(8,128)} %local.1) | copy-start | bytes 196612
  3.7 6.5 %copy-start.3 = (f32[8,2048]{1,0:T(8,128)S(1)}, f32[8,2048]{1,0:T(8,128)}, u32[]{:S(2)}) copy-start(f32[8,2048]{1,0:T(8,128)} %weight.1) | copy-start | bytes 196612
  3.8 5.4 %collective-permute-start.1 = (f32[32,128]{1,0:T(8,128)S(1)}, f32[32,128]{1,0:T(8,128)S(1)}, u32[]{:S(2)}, u32[]{:S(2)}) collective-permute-start(f32[32,128]{1,0:T(8,128)S(1)} %get-tuple-element.3), channel_id=1, source_target_pairs={{1,0},{2,1},{3,2},{4,3},{5,4},{6,5},{7,6},{9,8},{10,9},{11,10},{12... | collective-permute-start | bytes 49160 | tf_op jit(solution)/shard_map/ppermute | solution.py:25
  10.3 53.5 %copy-start = (f32[32,4096]{1,0:T(8,128)S(1)}, f32[32,4096]{1,0:T(8,128)}, u32[]{:S(2)}) copy-start(f32[32,4096]{1,0:T(8,128)} %probes.1) | copy-start | bytes 1572868
  10.3 53.5 %copy-start.4 = (f32[4096]{0:T(1024)S(1)}, f32[4096]{0:T(1024)}, u32[]{:S(2)}) copy-start(f32[4096]{0:T(1024)} %param.8) | copy-start | bytes 49156

commit v3 on v2

--- a/solution.py
+++ b/solution.py
@@ -14,19 +14,6 @@
 highest = lax.Precision.HIGHEST
 
 
-def extended_2(block, sides, width):
-    for axis, dim in sides:
-        count = lax.axis_size(axis)
-        forward = [(i, i + 1) for i in range(count - 1)]
-        backward = [(target, source) for source, target in forward]
-        low = lax.ppermute(
-            lax.slice_in_dim(block, block.shape[dim] - width, None, axis=dim), axis, forward
-        )
-        high = lax.ppermute(lax.slice_in_dim(block, 0, width, axis=dim), axis, backward)
-        block = jnp.concatenate([low, block, high], axis=dim)
-    return block
-
-
 TILE = 128
 WIDE = 256
 
@@ -39,40 +26,70 @@
     return high, middle, low
 
 
-def element_kernel(extended, local, sensitivity, weight, out, node, held, pulled, total):
+MESH = pl.DeviceIdType.MESH
+
+
+def element_kernel(
+    extended, local, corner_column, sensitivity, weight, out, node, spread, held, pulled, total
+):
     gauss_count, corner_count, element_count = sensitivity.shape
     rows, nodes = extended.shape
     tiles, wides = nodes // TILE, nodes // WIDE
+    blocks = element_count // WIDE
     total[...] = jnp.zeros_like(total)
 
-    def block(step, carry):
+    def load_nodes(step, turn):
         start = pl.multiple_of(step * WIDE, WIDE)
         for c in range(corner_count):
             index = local[c : c + 1, pl.ds(start, WIDE)]
-            node[c] = jnp.broadcast_to(index, (8, WIDE))
-
-        def gather(corner, carry):
-            for part in range(WIDE // TILE):
-                index = node[corner, :, part * TILE : (part + 1) * TILE]
-                lane, tile = index & (TILE - 1), index >> 7
-                found = [jnp.zeros((8, TILE), jnp.float32)] * (rows // 8)
-                for t in range(tiles):
-                    here = tile == t
-                    for r in range(rows // 8):
-                        source = extended[r * 8 : (r + 1) * 8, t * TILE : (t + 1) * TILE]
-                        picked = jnp.take_along_axis(
-                            source, lane, axis=1, mode="promise_in_bounds"
-                        )
-                        found[r] = jnp.where(here, picked, found[r])
-                for r in range(rows // 8):
-                    held[corner, r * 8 : (r + 1) * 8, part * TILE : (part + 1) * TILE] = found[r]
-            return carry
-
-        lax.fori_loop(0, corner_count, gather, 0)
-
+            node[turn, c] = jnp.broadcast_to(index, (16, WIDE))
+
+    def load_columns(step):
+        start = pl.multiple_of(step * WIDE, WIDE)
+        for c in range(corner_count):
+            column = corner_column[pl.ds(start, WIDE), c : c + 1]
+            spread[c] = jnp.broadcast_to(column & (WIDE - 1), (WIDE, TILE))
+
+    def gather(corner, turn):
         for part in range(WIDE // TILE):
             lanes = slice(part * TILE, (part + 1) * TILE)
-            place = pl.multiple_of(start + part * TILE, TILE)
+            index = node[turn, corner, 0:8, lanes]
+            lane, tile = index & (TILE - 1), index >> 7
+            found = [jnp.zeros((8, TILE), jnp.float32)] * (rows // 8)
+            for t in range(tiles):
+                here = tile == t
+                for r in range(rows // 8):
+                    source = extended[r * 8 : (r + 1) * 8, t * TILE : (t + 1) * TILE]
+                    picked = jnp.take_along_axis(source, lane, axis=1, mode="promise_in_bounds")
+                    found[r] = jnp.where(here, picked, found[r])
+            for r in range(rows // 8):
+                held[corner, r * 8 : (r + 1) * 8, lanes] = found[r]
+
+    def scatter(corner, turn):
+        wide = node[turn, corner] >> 8
+        lane = spread[corner]
+        count = lax.broadcasted_iota(jnp.int32, (WIDE, TILE), 1)
+        hot = jnp.concatenate(
+            [
+                jnp.where(lane == count + part * TILE, 1.0, 0.0).astype(jnp.bfloat16)
+                for part in range(WIDE // TILE)
+            ],
+            axis=1,
+        )
+        hot = jnp.concatenate([hot, hot, hot], axis=0)
+        value = jnp.concatenate(split_exact(pulled[corner]), axis=1)
+        masked = []
+        for h in range(wides):
+            mask = jnp.where(wide == h, 1.0, 0.0).astype(jnp.bfloat16)
+            mask = jnp.concatenate([mask] * (rows // 16), axis=0)
+            masked.append(value * jnp.concatenate([mask] * 3, axis=1))
+        masked = jnp.concatenate(masked, axis=0)
+        total[...] += jnp.dot(masked, hot, preferred_element_type=jnp.float32)
+
+    def elements(step):
+        for part in range(WIDE // TILE):
+            lanes = slice(part * TILE, (part + 1) * TILE)
+            place = pl.multiple_of(step * WIDE + part * TILE, TILE)
             for r in range(rows // 16):
                 band = slice(r * 16, (r + 1) * 16)
                 values = [held[c, band, lanes] for c in range(corner_count)]
@@ -91,29 +108,29 @@
                 for c in range(corner_count):
                     pulled[c, band, lanes] = sums[c]
 
-        def scatter(corner, carry):
-            index = node[corner, 0:1, :]
-            lane = jnp.broadcast_to(index & (WIDE - 1), (WIDE, WIDE))
-            wide = jnp.broadcast_to(index >> 8, (16, WIDE))
-            hot = jnp.where(lax.broadcasted_iota(jnp.int32, (WIDE, WIDE), 0) == lane, 1.0, 0.0)
-            hot = hot.astype(jnp.bfloat16)
-            hot = jnp.concatenate([hot, hot, hot], axis=1)
-            value = jnp.concatenate(split_exact(pulled[corner]), axis=1)
-            masked = []
-            for h in range(wides):
-                mask = jnp.where(wide == h, 1.0, 0.0).astype(jnp.bfloat16)
-                mask = jnp.concatenate([mask] * (rows // 16), axis=0)
-                masked.append(value * jnp.concatenate([mask] * 3, axis=1))
-            masked = jnp.concatenate(masked, axis=0)
-            total[...] += lax.dot_general(
-                masked, hot, (((1,), (1,)), ((), ())), preferred_element_type=jnp.float32
-            )
+    load_nodes(0, 0)
+
+    def first(corner, carry):
+        gather(corner, 0)
+        return carry
+
+    lax.fori_loop(0, corner_count, first, 0)
+
+    def block(step, carry):
+        turn = lax.rem(step, 2)
+        elements(step)
+        load_columns(step)
+        load_nodes(jnp.minimum(step + 1, blocks - 1), 1 - turn)
+
+        def both(corner, carry):
+            scatter(corner, turn)
+            gather(corner, 1 - turn)
             return carry
 
-        lax.fori_loop(0, corner_count, scatter, 0)
+        lax.fori_loop(0, corner_count, both, 0)
         return carry
 
-    lax.fori_loop(0, element_count // WIDE, block, 0)
+    lax.fori_loop(0, blocks, block, 0)
     for h in range(wides):
         out[:, h * WIDE : (h + 1) * WIDE] = total[h * rows : (h + 1) * rows, :]
 
@@ -126,32 +143,102 @@
 
 
 def element_images(extended, sensitivity, obs_weight, local):
-    probe_count, node_count = extended.shape
     corner_count = local.shape[0]
-    extended = padded(padded(extended, 0, 16), 1, WIDE)
     local = padded(local, 1, WIDE)
     sensitivity = padded(sensitivity, 2, WIDE)
     obs_weight = padded(obs_weight, 1, WIDE)
     rows, nodes = extended.shape
     vmem = pl.BlockSpec(memory_space=pltpu.VMEM)
-    summed = pl.pallas_call(
+    return pl.pallas_call(
         element_kernel,
         out_shape=jax.ShapeDtypeStruct((rows, nodes), jnp.float32),
-        in_specs=[vmem] * 4,
+        in_specs=[vmem] * 5,
         out_specs=vmem,
         scratch_shapes=[
-            pltpu.VMEM((corner_count, 8, WIDE), jnp.int32),
+            pltpu.VMEM((2, corner_count, 16, WIDE), jnp.int32),
+            pltpu.VMEM((corner_count, WIDE, TILE), jnp.int32),
             pltpu.VMEM((corner_count, rows, WIDE), jnp.float32),
             pltpu.VMEM((corner_count, rows, WIDE), jnp.float32),
             pltpu.VMEM((nodes // WIDE * rows, WIDE), jnp.float32),
         ],
         compiler_params=pltpu.CompilerParams(vmem_limit_bytes=48 * 1024 * 1024),
         name="elements",
-    )(extended, local, sensitivity, obs_weight)
-    return summed[:probe_count, :node_count]
-
-
-MESH = pl.DeviceIdType.MESH
+    )(extended, local, local.T, sensitivity, obs_weight)
+
+
+def halo_kernel(space_axis_size, halo, probes, extended, send_sem, recv_sem):
+    s_me = lax.axis_index("space")
+    rows, nodes = probes.shape
+    has_lower, has_upper = s_me > 0, s_me < space_axis_size - 1
+    barrier = pltpu.get_barrier_semaphore()
+
+    def greet(to):
+        pl.semaphore_signal(barrier, inc=1, device_id={"space": to}, device_id_type=MESH)
+
+    pl.when(has_lower)(lambda: greet(s_me - 1))
+    pl.when(has_upper)(lambda: greet(s_me + 1))
+    pl.semaphore_wait(barrier, jnp.where(has_lower, 1, 0) + jnp.where(has_upper, 1, 0))
+
+    def copy(side):
+        low = side == 0
+        return pltpu.make_async_remote_copy(
+            src_ref=probes.at[:, :halo] if low else probes.at[:, nodes - halo :],
+            dst_ref=extended.at[:rows, halo + nodes : halo + nodes + halo]
+            if low
+            else extended.at[:rows, :halo],
+            send_sem=send_sem.at[side],
+            recv_sem=recv_sem.at[side],
+            device_id={"space": s_me - 1 if low else s_me + 1},
+            device_id_type=MESH,
+        )
+
+    pl.when(has_lower)(lambda: copy(0).start())
+    pl.when(has_upper)(lambda: copy(1).start())
+    extended[:rows, halo : halo + nodes] = probes[...]
+    if extended.shape[0] > rows:
+        extended[rows:, :] = jnp.zeros_like(extended[rows:, :])
+    end = halo + nodes + halo
+    if extended.shape[1] > end:
+        extended[:rows, end:] = jnp.zeros_like(extended[:rows, end:])
+
+    @pl.when(jnp.logical_not(has_lower))
+    def _():
+        extended[:rows, :halo] = jnp.zeros((rows, halo), jnp.float32)
+
+    @pl.when(jnp.logical_not(has_upper))
+    def _():
+        extended[:rows, halo + nodes : end] = jnp.zeros((rows, halo), jnp.float32)
+
+    @pl.when(has_lower)
+    def _():
+        copy(1).wait_recv()
+        copy(0).wait_send()
+
+    @pl.when(has_upper)
+    def _():
+        copy(0).wait_recv()
+        copy(1).wait_send()
+
+
+def with_halo(probes, halo):
+    space_axis_size = lax.axis_size("space")
+    rows, nodes = probes.shape
+    vmem = pl.BlockSpec(memory_space=pltpu.VMEM)
+    return pl.pallas_call(
+        functools.partial(halo_kernel, space_axis_size, halo),
+        out_shape=jax.ShapeDtypeStruct(
+            (rows + -rows % 16, nodes + 2 * halo + -(nodes + 2 * halo) % WIDE), jnp.float32
+        ),
+        in_specs=[vmem],
+        out_specs=vmem,
+        scratch_shapes=[pltpu.SemaphoreType.DMA((2,)), pltpu.SemaphoreType.DMA((2,))],
+        compiler_params=pltpu.CompilerParams(
+            collective_id=1, has_side_effects=True, vmem_limit_bytes=16 * 1024 * 1024
+        ),
+        name="halo",
+    )(probes)
+
+
 BAND = 8
 
 
@@ -249,7 +336,7 @@
 
 
 def orthonormal_kernel(
-    probe_axis_size, space_axis_size, summed, probes, prior, basis, factor,
+    probe_axis_size, space_axis_size, halo, summed, probes, prior, basis, factor,
     images, rim, mine, block, ready, partial, strips, bands, grams,
     rim_send, rim_recv, move_send, move_recv, a_send, a_recv, b_send, b_recv, c_send, c_recv,
 ):
@@ -258,7 +345,6 @@
     size = rows * probe_axis_size
     share = nodes // probe_axis_size
     strip = size // space_axis_size
-    halo = (summed.shape[1] - nodes) // 2
     scale = math.sqrt(float(nodes * space_axis_size))
 
     barrier = pltpu.get_barrier_semaphore()
@@ -270,8 +356,10 @@
         pl.semaphore_signal(barrier, inc=1, device_id={"probe": to}, device_id_type=MESH)
     pl.semaphore_wait(barrier, space_axis_size + probe_axis_size - 2)
 
+    end = halo + nodes + halo
+
     def rim_copy(side):
-        source = summed.at[:, :halo] if side == 0 else summed.at[:, halo + nodes :]
+        source = summed.at[:rows, :halo] if side == 0 else summed.at[:rows, halo + nodes : end]
         return pltpu.make_async_remote_copy(
             src_ref=source,
             dst_ref=rim.at[side],
@@ -284,7 +372,7 @@
     has_lower, has_upper = s_me > 0, s_me < space_axis_size - 1
     pl.when(has_lower)(lambda: rim_copy(0).start())
     pl.when(has_upper)(lambda: rim_copy(1).start())
-    images[...] = summed[:, halo : halo + nodes] + prior[...] * probes[...]
+    images[...] = summed[:rows, halo : halo + nodes] + prior[...] * probes[...]
 
     @pl.when(has_upper)
     def _():
@@ -353,16 +441,15 @@
     pl.when(has_upper)(lambda: rim_copy(1).wait_send())
 
 
-def orthonormal(summed, probes, prior):
+def orthonormal(summed, probes, prior, halo):
     probe_axis_size, space_axis_size = lax.axis_size("probe"), lax.axis_size("space")
     rows, nodes = probes.shape
-    halo = (summed.shape[1] - nodes) // 2
     size, share = rows * probe_axis_size, nodes // probe_axis_size
     strip = size // space_axis_size
     vmem = pl.BlockSpec(memory_space=pltpu.VMEM)
     dma = pltpu.SemaphoreType.DMA
     return pl.pallas_call(
-        functools.partial(orthonormal_kernel, probe_axis_size, space_axis_size),
+        functools.partial(orthonormal_kernel, probe_axis_size, space_axis_size, halo),
         out_shape=(
             jax.ShapeDtypeStruct((rows, nodes), jnp.float32),
             jax.ShapeDtypeStruct((size, size), jnp.float32),
@@ -398,9 +485,9 @@
 
 
 def on_device(probes, sensitivity, obs_weight, prior_weight, connectivity):
-    extended = extended_2(probes, (("space", 1),), HALO)
+    extended = with_halo(probes, HALO)
     summed = element_images(extended, sensitivity, obs_weight, connectivity)
-    return orthonormal(summed, probes, prior_weight[None, :])
+    return orthonormal(summed, probes, prior_weight[None, :], HALO)
 
 
 def solution(mesh):

time: 128 us -> 105 us (0.82)
  Pallas kernels: 116 us -> 101 us
  waiting for transfers between devices: 3.96 us -> 0 us
  starting transfers between devices: 3.77 us -> 0 us
  local copies, waits for them, and re-layouts: 2.2 us -> 3.5 us
    pallas_call x1, Pallas kernels: 53.4 us -> 33.9 us  [element_images(): pl.pallas_call(element_kernel, out_shape=jax.ShapeDtypeStruct((rows, node...]
    ppermute x2 -> x0, waiting for transfers between devices: 3.96 us -> none  [the longest x1 3.96 us: extended_2(): lax.ppermute(lax.slice_in_dim(block, 0, width, axis=dim), axis, backward)]
    pallas_call x0 -> x1, Pallas kernels: none -> 3.85 us  [with_halo(): pl.pallas_call(functools.partial(halo_kernel, space_axis_size, halo), out...]
    ppermute x2 -> x0, starting transfers between devices: 3.77 us -> none  [the longest x1 2.35 us: extended_2(): lax.ppermute(lax.slice_in_dim(block, block.shape[dim] - width, None, axis...]
    unnamed x12 -> x15, local copies, waits for them, and re-layouts: 1.46 us -> 3.5 us
  transfers between devices with their start and end apart: 2 -> 0, of which waited for: 1 -> 0; matrix products, arithmetic and copies ran while one was open for 0% -> 0% of each run, Pallas kernels for 0% -> 0%
where the time goes in v3:
time: 105 us
  Pallas kernels  101 us (96%)
  local copies, waits for them, and re-layouts  3.5 us (3%)
    pallas_call x1, Pallas kernels, orthonormal(): pl.pallas_call(functools.partial(orthonormal_kernel, probe_axis_size, spa...  62.8 us
    pallas_call x1, Pallas kernels, element_images(): pl.pallas_call(element_kernel, out_shape=jax.ShapeDtypeStruct((rows, node...  33.9 us
    pallas_call x1, Pallas kernels, with_halo(): pl.pallas_call(functools.partial(halo_kernel, space_axis_size, halo), out...  3.85 us
    unnamed x15, local copies, waits for them, and re-layouts  3.5 us

profile of v3, /device:TPU:0, one launch (start us, length us, event | category | flops | bytes accessed | tf_op | source)
XLA Modules:
  0.0 104.8 jit_solution(17257609640603097025)
XLA Ops:
  0.6 0.0 copy-start
  0.6 1.0 copy-done
  1.7 0.0 copy-start.3
  1.7 3.8 %halo.1.extended = f32[32,4352]{1,0:T(8,128)S(1)} custom-call(f32[32,4096]{1,0:T(8,128)S(1)} %copy-done), custom_call_target="tpu_custom_call" | custom-call | tf_op jit(solution)/shard_map/halo/pallas_call | solution.py:227
  5.5 0.0 copy-done.3
  5.5 0.0 copy-start.2
  5.6 0.0 copy-start.4
  5.6 0.3 copy.7
  5.9 0.7 copy-done.2
  6.6 0.0 copy-done.4
  6.6 0.0 copy-start.1
  6.6 0.0 copy-start.5
  6.6 33.9 %elements.1.summed = f32[32,4352]{1,0:T(8,128)S(1)} custom-call(f32[32,4352]{1,0:T(8,128)S(1)} %halo.1.extended, s32[8,2048]{1,0:T(8,128)S(1)} %copy-done.3, s32[2048,8]{1,0:T(8,128)S(1)} %bitcast.2, f32[8,8,2048]{2,1,0:T(8,128)S(1)} %copy-done.2, f32[8,2048]{1,0:T(8,128)S(1)} %copy-done.4), custom_call_target="tpu_custom_call" | custom-call | tf_op jit(solution)/shard_map/elements/pallas_call | solution.py:152
  40.5 0.0 copy-done.1
  40.6 0.0 copy-done.5
  40.6 62.8 %orthonormal.1 = (f32[32,4096]{1,0:T(8,128)S(1)}, f32[128,128]{1,0:T(8,128)S(1)}) custom-call(f32[32,4352]{1,0:T(8,128)S(1)} %elements.1.summed, f32[32,4096]{1,0:T(8,128)S(1)} %copy-done.1, f32[1,4096]{1,0:T(1,128)S(1)} %bitcast.3), custom_call_target="tpu_custom_call" | custom-call | tf_op jit(solution)/shard_map/orthonormal/pallas_call | solution.py:451
  103.4 0.8 copy.10
  104.2 0.6 copy.11
Async XLA Ops:
  0.6 1.0 copy-start
  1.7 3.9 %copy-start.3 = (s32[8,2048]{1,0:T(8,128)S(1)}, s32[8,2048]{1,0:T(8,128)}, u32[]{:S(2)}) copy-start(s32[8,2048]{1,0:T(8,128)} %local.1) | copy-start | bytes 196612
  5.5 1.0 copy-start.2
  5.6 1.0 copy-start.4
  6.6 34.0 %copy-start.1 = (f32[32,4096]{1,0:T(8,128)S(1)}, f32[32,4096]{1,0:T(8,128)}, u32[]{:S(2)}) copy-start(f32[32,4096]{1,0:T(8,128)} %probes.3) | copy-start | bytes 1572868
  6.6 34.0 %copy-start.5 = (f32[4096]{0:T(1024)S(1)}, f32[4096]{0:T(1024)}, u32[]{:S(2)}) copy-start(f32[4096]{0:T(1024)} %param.8) | copy-start | bytes 49156

commit v4 on v3

--- a/solution.py
+++ b/solution.py
@@ -252,11 +252,8 @@
     )
 
 
-def small_factor(columns):
-    entry = {}
-    for m in range(BAND):
-        for i in range(m, BAND):
-            entry[i, m] = jnp.broadcast_to(columns[m][i : i + 1, :], columns[m].shape)
+def small_factor(entry):
+    entry = dict(entry)
     inverse = {}
     for m in range(BAND):
         root = lax.rsqrt(entry[m, m])
@@ -274,23 +271,40 @@
     return inverse
 
 
+def lane_columns(band, start):
+    return [
+        jnp.broadcast_to(band[:, start + m : start + m + 1], band.shape) for m in range(BAND)
+    ]
+
+
+def row_sum(value):
+    return jnp.broadcast_to(jnp.sum(value, axis=0, keepdims=True), value.shape)
+
+
+def block_entries(band, start):
+    columns = lane_columns(band, start)
+    return {
+        (i, m): jnp.broadcast_to(columns[m][i : i + 1, :], band.shape)
+        for m in range(BAND)
+        for i in range(m, BAND)
+    }
+
+
 def factored(gram):
     size = gram.shape[0]
     row = lax.broadcasted_iota(jnp.int32, (size, size), 0)
     column = lax.broadcasted_iota(jnp.int32, (size, size), 1)
     unit = jnp.where(row == column, 1.0, 0.0)
     level = lax.broadcasted_iota(jnp.int32, (BAND, size), 0)
+    count = size // BAND
     bands = []
-    for j in range(size // BAND):
+    for j in range(count):
         part = slice(j * BAND, (j + 1) * BAND)
         bands.append((gram[part], unit[part]))
-    for j in range(size // BAND):
+    entry = block_entries(bands[0][0], 0)
+    for j in range(count):
         left, right = bands[j]
-        columns = [
-            jnp.broadcast_to(left[:, j * BAND + m : j * BAND + m + 1], left.shape)
-            for m in range(BAND)
-        ]
-        inverse = small_factor(columns)
+        inverse = small_factor(entry)
         new_left = new_right = None
         for m in range(BAND):
             weights = jnp.zeros_like(left)
@@ -301,11 +315,21 @@
             new_left = add_left if m == 0 else new_left + add_left
             new_right = add_right if m == 0 else new_right + add_right
         bands[j] = (new_left, new_right)
-        if (j + 1) * BAND < size:
+        if j + 1 < count:
+            columns = lane_columns(new_left, (j + 1) * BAND)
+            left, right = bands[j + 1]
+            entry = block_entries(left, (j + 1) * BAND)
+            for i, m in entry:
+                entry[i, m] = entry[i, m] - row_sum(columns[i] * columns[m])
+            for i in range(BAND):
+                left = jnp.where(level == i, left - row_sum(columns[i] * new_left), left)
+                right = jnp.where(level == i, right - row_sum(columns[i] * new_right), right)
+            bands[j + 1] = (left, right)
+        if j + 2 < count:
             multipliers = new_left.T
             away_left = exact_dot(multipliers, new_left)
             away_right = exact_dot(multipliers, new_right)
-            for i in range(j + 1, size // BAND):
+            for i in range(j + 2, count):
                 part = slice(i * BAND, (i + 1) * BAND)
                 bands[i] = (bands[i][0] - away_left[part], bands[i][1] - away_right[part])
     upper = jnp.concatenate([band[0] for band in bands], axis=0)
@@ -337,8 +361,8 @@
 
 def orthonormal_kernel(
     probe_axis_size, space_axis_size, halo, summed, probes, prior, basis, factor,
-    images, rim, mine, block, ready, partial, strips, bands, grams,
-    rim_send, rim_recv, move_send, move_recv, a_send, a_recv, b_send, b_recv, c_send, c_recv,
+    images, rim, mine, block, everything, rows_of, partial, strips, bands, grams,
+    rim_send, rim_recv, move_send, move_recv, rest_send, rest_recv, a_send, a_recv, b_send, b_recv, c_send, c_recv,
 ):
     p_me, s_me = lax.axis_index("probe"), lax.axis_index("space")
     rows, nodes = probes.shape
@@ -389,7 +413,7 @@
 
     copies = send_all(
         "probe", probe_axis_size, p_me, lambda to: images.at[:, lanes(to)],
-        mine.at[p_me], move_send.at[0], move_recv.at[0],
+        mine.at[p_me], move_send, move_recv,
     )
     mine[p_me] = images[:, lanes(p_me)]
     wait_all(copies)
@@ -424,19 +448,35 @@
         return jnp.concatenate([grams[turn, s] for s in range(space_axis_size)], axis=0)
 
     whole = mine[...].reshape(size, share)
-    upper_first, inverse_first = factored(summed_gram(0, exact_dot(whole, whole, 1, 1)))
+    gram_first = summed_gram(0, exact_dot(whole, whole, 1, 1))
+    rest = []
+    for e in range(1, probe_axis_size):
+        for d in range(1, probe_axis_size):
+            to = lax.rem(p_me + d, probe_axis_size)
+            place = lanes(lax.rem(to + e, probe_axis_size))
+            copy = pltpu.make_async_remote_copy(
+                src_ref=images.at[:, place],
+                dst_ref=everything.at[p_me, :, place],
+                send_sem=rest_send.at[d, e],
+                recv_sem=rest_recv.at[d, e],
+                device_id={"probe": to},
+                device_id_type=MESH,
+            )
+            copy.start()
+            rest.append(copy)
+    everything[:, :, lanes(p_me)] = mine[...]
+    for e in range(1, probe_axis_size):
+        place = lanes(lax.rem(p_me + e, probe_axis_size))
+        everything[p_me, :, place] = images[:, place]
+    upper_first, inverse_first = factored(gram_first)
     block[...] = exact_dot(inverse_first, mine[...].reshape(size, share))
     first = block[...]
     upper_second, inverse_second = factored(summed_gram(1, exact_dot(first, first, 1, 1)))
-    done = exact_dot(inverse_second * scale, block[...])
-    ready[...] = done.reshape(probe_axis_size, rows, share)
-    copies = send_all(
-        "probe", probe_axis_size, p_me, lambda to: ready.at[to],
-        basis.at[:, lanes(p_me)], move_send.at[1], move_recv.at[1],
-    )
-    basis[:, lanes(p_me)] = ready[p_me]
     factor[...] = exact_dot(upper_second, upper_first) / scale
-    wait_all(copies)
+    rows_of[...] = exact_dot(inverse_second * scale, inverse_first)
+    own = rows_of[pl.ds(pl.multiple_of(p_me * rows, rows), rows), :]
+    wait_all(rest)
+    basis[...] = exact_dot(own, everything[...].reshape(size, nodes))
     pl.when(has_lower)(lambda: rim_copy(0).wait_send())
     pl.when(has_upper)(lambda: rim_copy(1).wait_send())
 
@@ -461,15 +501,18 @@
             pltpu.VMEM((2, rows, halo), jnp.float32),
             pltpu.VMEM((probe_axis_size, rows, share), jnp.float32),
             pltpu.VMEM((size, share), jnp.float32),
-            pltpu.VMEM((probe_axis_size, rows, share), jnp.float32),
+            pltpu.VMEM((probe_axis_size, rows, nodes), jnp.float32),
+            pltpu.VMEM((size, size), jnp.float32),
             pltpu.VMEM((2, space_axis_size, strip, size), jnp.float32),
             pltpu.VMEM((2, space_axis_size, strip, size), jnp.float32),
             pltpu.VMEM((2, probe_axis_size, strip, size), jnp.float32),
             pltpu.VMEM((2, space_axis_size, strip, size), jnp.float32),
             dma((2,)),
             dma((2,)),
-            dma((2, probe_axis_size)),
-            dma((2, probe_axis_size)),
+            dma((probe_axis_size,)),
+            dma((probe_axis_size,)),
+            dma((probe_axis_size, probe_axis_size)),
+            dma((probe_axis_size, probe_axis_size)),
             dma((2, space_axis_size)),
             dma((2, space_axis_size)),
             dma((2, probe_axis_size)),

time: 105 us -> 103 us (0.981)
  Pallas kernels: 101 us -> 98.2 us
    pallas_call x1, Pallas kernels: 62.8 us -> 60.4 us  [orthonormal(): pl.pallas_call(functools.partial(orthonormal_kernel, probe_axis_size, spa...]
where the time goes in v4:
time: 103 us; the launch traced here: 102 us
  Pallas kernels  98.2 us (95%)
  local copies, waits for them, and re-layouts  3.5 us (3%)
    pallas_call x1, Pallas kernels, orthonormal(): pl.pallas_call(functools.partial(orthonormal_kernel, probe_axis_size, spa...  60.4 us
    pallas_call x1, Pallas kernels, element_images(): pl.pallas_call(element_kernel, out_shape=jax.ShapeDtypeStruct((rows, node...  33.9 us
    pallas_call x1, Pallas kernels, with_halo(): pl.pallas_call(functools.partial(halo_kernel, space_axis_size, halo), out...  3.85 us
    unnamed x15, local copies, waits for them, and re-layouts  3.5 us

profile of v4, /device:TPU:0, one launch (start us, length us, event | category | flops | bytes accessed | tf_op | source)
XLA Modules:
  0.0 102.4 jit_solution(6663780926416482482)
XLA Ops:
  0.6 0.0 copy-start
  0.6 1.0 %copy-done = f32[32,4096]{1,0:T(8,128)S(1)} copy-done((f32[32,4096]{1,0:T(8,128)S(1)}, f32[32,4096]{1,0:T(8,128)}, u32[]{:S(2)}) %copy-start) | copy-done | bytes 524312
  1.7 0.0 copy-start.3
  1.7 3.8 %halo.1.extended = f32[32,4352]{1,0:T(8,128)S(1)} custom-call(f32[32,4096]{1,0:T(8,128)S(1)} %copy-done), custom_call_target="tpu_custom_call" | custom-call | tf_op jit(solution)/shard_map/halo/pallas_call | solution.py:227
  5.5 0.0 copy-done.3
  5.5 0.0 copy-start.2
  5.6 0.0 copy-start.4
  5.6 0.3 copy.7
  5.9 0.7 copy-done.2
  6.6 0.0 copy-done.4
  6.6 0.0 copy-start.1
  6.6 0.0 copy-start.5
  6.6 33.9 %elements.1.summed = f32[32,4352]{1,0:T(8,128)S(1)} custom-call(f32[32,4352]{1,0:T(8,128)S(1)} %halo.1.extended, s32[8,2048]{1,0:T(8,128)S(1)} %copy-done.3, s32[2048,8]{1,0:T(8,128)S(1)} %bitcast.2, f32[8,8,2048]{2,1,0:T(8,128)S(1)} %copy-done.2, f32[8,2048]{1,0:T(8,128)S(1)} %copy-done.4), custom_call_target="tpu_custom_call" | custom-call | tf_op jit(solution)/shard_map/elements/pallas_call | solution.py:152
  40.5 0.0 copy-done.1
  40.6 0.0 copy-done.5
  40.6 60.4 %orthonormal.1 = (f32[32,4096]{1,0:T(8,128)S(1)}, f32[128,128]{1,0:T(8,128)S(1)}) custom-call(f32[32,4352]{1,0:T(8,128)S(1)} %elements.1.summed, f32[32,4096]{1,0:T(8,128)S(1)} %copy-done.1, f32[1,4096]{1,0:T(1,128)S(1)} %bitcast.3), custom_call_target="tpu_custom_call" | custom-call | tf_op jit(solution)/shard_map/orthonormal/pallas_call | solution.py:491
  101.0 0.8 copy.10
  101.8 0.6 copy.11
Async XLA Ops:
  0.6 1.0 %copy-start = (f32[32,4096]{1,0:T(8,128)S(1)}, f32[32,4096]{1,0:T(8,128)}, u32[]{:S(2)}) copy-start(f32[32,4096]{1,0:T(8,128)} %probes.3) | copy-start | bytes 1572868
  1.7 3.9 %copy-start.3 = (s32[8,2048]{1,0:T(8,128)S(1)}, s32[8,2048]{1,0:T(8,128)}, u32[]{:S(2)}) copy-start(s32[8,2048]{1,0:T(8,128)} %local.1) | copy-start | bytes 196612
  5.5 1.0 %copy-start.2 = (f32[8,8,2048]{2,1,0:T(8,128)S(1)}, f32[8,8,2048]{2,1,0:T(8,128)}, u32[]{:S(2)}) copy-start(f32[8,8,2048]{2,1,0:T(8,128)} %sensitivity.1) | copy-start | bytes 1572868
  5.6 1.0 %copy-start.4 = (f32[8,2048]{1,0:T(8,128)S(1)}, f32[8,2048]{1,0:T(8,128)}, u32[]{:S(2)}) copy-start(f32[8,2048]{1,0:T(8,128)} %weight.1) | copy-start | bytes 196612
  6.6 34.0 %copy-start.1 = (f32[32,4096]{1,0:T(8,128)S(1)}, f32[32,4096]{1,0:T(8,128)}, u32[]{:S(2)}) copy-start(f32[32,4096]{1,0:T(8,128)} %probes.3) | copy-start | bytes 1572868
  6.6 34.0 %copy-start.5 = (f32[4096]{0:T(1024)S(1)}, f32[4096]{0:T(1024)}, u32[]{:S(2)}) copy-start(f32[4096]{0:T(1024)} %param.8) | copy-start | bytes 49156

commit v5 on v4

--- a/solution.py
+++ b/solution.py
@@ -36,6 +36,7 @@
     rows, nodes = extended.shape
     tiles, wides = nodes // TILE, nodes // WIDE
     blocks = element_count // WIDE
+    together = math.gcd(corner_count, 4)
     total[...] = jnp.zeros_like(total)
 
     def load_nodes(step, turn):
@@ -65,7 +66,7 @@
             for r in range(rows // 8):
                 held[corner, r * 8 : (r + 1) * 8, lanes] = found[r]
 
-    def scatter(corner, turn):
+    def scatter_terms(corner, turn):
         wide = node[turn, corner] >> 8
         lane = spread[corner]
         count = lax.broadcasted_iota(jnp.int32, (WIDE, TILE), 1)
@@ -83,7 +84,12 @@
             mask = jnp.where(wide == h, 1.0, 0.0).astype(jnp.bfloat16)
             mask = jnp.concatenate([mask] * (rows // 16), axis=0)
             masked.append(value * jnp.concatenate([mask] * 3, axis=1))
-        masked = jnp.concatenate(masked, axis=0)
+        return jnp.concatenate(masked, axis=0), hot
+
+    def scatter(corners, turn):
+        terms = [scatter_terms(corner, turn) for corner in corners]
+        masked = jnp.concatenate([term[0] for term in terms], axis=1)
+        hot = jnp.concatenate([term[1] for term in terms], axis=0)
         total[...] += jnp.dot(masked, hot, preferred_element_type=jnp.float32)
 
     def elements(step):
@@ -122,12 +128,14 @@
         load_columns(step)
         load_nodes(jnp.minimum(step + 1, blocks - 1), 1 - turn)
 
-        def both(corner, carry):
-            scatter(corner, turn)
-            gather(corner, 1 - turn)
+        def both(step, carry):
+            corners = [step * together + c for c in range(together)]
+            scatter(corners, turn)
+            for corner in corners:
+                gather(corner, 1 - turn)
             return carry
 
-        lax.fori_loop(0, corner_count, both, 0)
+        lax.fori_loop(0, corner_count // together, both, 0)
         return carry
 
     lax.fori_loop(0, blocks, block, 0)
@@ -398,6 +406,27 @@
     pl.when(has_upper)(lambda: rim_copy(1).start())
     images[...] = summed[:rows, halo : halo + nodes] + prior[...] * probes[...]
 
+    def lanes(index):
+        return pl.ds(pl.multiple_of(index * share, share), share)
+
+    def quarter_copy(d):
+        to = lax.rem(p_me + d, probe_axis_size)
+        return pltpu.make_async_remote_copy(
+            src_ref=images.at[:, lanes(to)],
+            dst_ref=mine.at[p_me],
+            send_sem=move_send.at[d],
+            recv_sem=move_recv.at[d],
+            device_id={"probe": to},
+            device_id_type=MESH,
+        )
+
+    def at_rim(d):
+        to = lax.rem(p_me + d, probe_axis_size)
+        return jnp.logical_or(to == 0, to == probe_axis_size - 1)
+
+    for d in range(1, probe_axis_size):
+        pl.when(jnp.logical_not(at_rim(d)))(lambda d=d: quarter_copy(d).start())
+
     @pl.when(has_upper)
     def _():
         rim_copy(0).wait_recv()
@@ -408,15 +437,11 @@
         rim_copy(1).wait_recv()
         images[:, :halo] += rim[1]
 
-    def lanes(index):
-        return pl.ds(pl.multiple_of(index * share, share), share)
-
-    copies = send_all(
-        "probe", probe_axis_size, p_me, lambda to: images.at[:, lanes(to)],
-        mine.at[p_me], move_send, move_recv,
-    )
+    for d in range(1, probe_axis_size):
+        pl.when(at_rim(d))(lambda d=d: quarter_copy(d).start())
     mine[p_me] = images[:, lanes(p_me)]
-    wait_all(copies)
+    for d in range(1, probe_axis_size):
+        quarter_copy(d).wait()
 
     def summed_gram(turn, value):
         for s in range(space_axis_size):

time: 103 us -> 98.5 us (0.956)
  Pallas kernels: 98.2 us -> 94.1 us
    pallas_call x1, Pallas kernels: 33.9 us -> 29.7 us  [element_images(): pl.pallas_call(element_kernel, out_shape=jax.ShapeDtypeStruct((rows, node...]
where the time goes in v5:
time: 98.5 us; the launch traced here: 98.3 us
  Pallas kernels  94.1 us (96%)
  local copies, waits for them, and re-layouts  3.5 us (4%)
    pallas_call x1, Pallas kernels, orthonormal(): pl.pallas_call(functools.partial(orthonormal_kernel, probe_axis_size, spa...  60.6 us
    pallas_call x1, Pallas kernels, element_images(): pl.pallas_call(element_kernel, out_shape=jax.ShapeDtypeStruct((rows, node...  29.7 us
    pallas_call x1, Pallas kernels, with_halo(): pl.pallas_call(functools.partial(halo_kernel, space_axis_size, halo), out...  3.85 us
    unnamed x15, local copies, waits for them, and re-layouts  3.5 us

profile of v5, /device:TPU:0, one launch (start us, length us, event | category | flops | bytes accessed | tf_op | source)
XLA Modules:
  0.0 98.3 jit_solution(10459106768227752273)
XLA Ops:
  0.6 0.0 copy-start
  0.6 1.0 %copy-done = f32[32,4096]{1,0:T(8,128)S(1)} copy-done((f32[32,4096]{1,0:T(8,128)S(1)}, f32[32,4096]{1,0:T(8,128)}, u32[]{:S(2)}) %copy-start) | copy-done | bytes 524312
  1.7 0.0 copy-start.3
  1.7 3.8 %halo.1.extended = f32[32,4352]{1,0:T(8,128)S(1)} custom-call(f32[32,4096]{1,0:T(8,128)S(1)} %copy-done), custom_call_target="tpu_custom_call" | custom-call | tf_op jit(solution)/shard_map/halo/pallas_call | solution.py:235
  5.5 0.0 copy-done.3
  5.5 0.0 copy-start.2
  5.6 0.0 copy-start.4
  5.6 0.3 copy.7
  5.9 0.7 copy-done.2
  6.6 0.0 copy-done.4
  6.6 0.0 copy-start.1
  6.6 0.0 copy-start.5
  6.6 29.7 %elements.1.summed = f32[32,4352]{1,0:T(8,128)S(1)} custom-call(f32[32,4352]{1,0:T(8,128)S(1)} %halo.1.extended, s32[8,2048]{1,0:T(8,128)S(1)} %copy-done.3, s32[2048,8]{1,0:T(8,128)S(1)} %bitcast.2, f32[8,8,2048]{2,1,0:T(8,128)S(1)} %copy-done.2, f32[8,2048]{1,0:T(8,128)S(1)} %copy-done.4), custom_call_target="tpu_custom_call" | custom-call | tf_op jit(solution)/shard_map/elements/pallas_call | solution.py:160
  36.3 0.0 copy-done.1
  36.3 0.0 copy-done.5
  36.3 60.6 %orthonormal.1 = (f32[32,4096]{1,0:T(8,128)S(1)}, f32[128,128]{1,0:T(8,128)S(1)}) custom-call(f32[32,4352]{1,0:T(8,128)S(1)} %elements.1.summed, f32[32,4096]{1,0:T(8,128)S(1)} %copy-done.1, f32[1,4096]{1,0:T(1,128)S(1)} %bitcast.3), custom_call_target="tpu_custom_call" | custom-call | tf_op jit(solution)/shard_map/orthonormal/pallas_call | solution.py:516
  96.9 0.8 copy.10
  97.7 0.6 copy.11
Async XLA Ops:
  0.6 1.0 %copy-start = (f32[32,4096]{1,0:T(8,128)S(1)}, f32[32,4096]{1,0:T(8,128)}, u32[]{:S(2)}) copy-start(f32[32,4096]{1,0:T(8,128)} %probes.3) | copy-start | bytes 1572868
  1.7 3.9 %copy-start.3 = (s32[8,2048]{1,0:T(8,128)S(1)}, s32[8,2048]{1,0:T(8,128)}, u32[]{:S(2)}) copy-start(s32[8,2048]{1,0:T(8,128)} %local.1) | copy-start | bytes 196612
  5.5 1.0 %copy-start.2 = (f32[8,8,2048]{2,1,0:T(8,128)S(1)}, f32[8,8,2048]{2,1,0:T(8,128)}, u32[]{:S(2)}) copy-start(f32[8,8,2048]{2,1,0:T(8,128)} %sensitivity.1) | copy-start | bytes 1572868
  5.6 1.0 %copy-start.4 = (f32[8,2048]{1,0:T(8,128)S(1)}, f32[8,2048]{1,0:T(8,128)}, u32[]{:S(2)}) copy-start(f32[8,2048]{1,0:T(8,128)} %weight.1) | copy-start | bytes 196612
  6.6 29.7 %copy-start.1 = (f32[32,4096]{1,0:T(8,128)S(1)}, f32[32,4096]{1,0:T(8,128)}, u32[]{:S(2)}) copy-start(f32[32,4096]{1,0:T(8,128)} %probes.3) | copy-start | bytes 1572868
  6.6 29.7 %copy-start.5 = (f32[4096]{0:T(1024)S(1)}, f32[4096]{0:T(1024)}, u32[]{:S(2)}) copy-start(f32[4096]{0:T(1024)} %param.8) | copy-start | bytes 49156
